TPU v7x, 32 devices: a whole 2x2x4 slice. The times are simulated.
32 devices in a mesh: sub: 8 (over z, x), blk: 4 (over y, core).
Axes of the slice: x: 2, y: 2, z: 4, core: 2. Of those that a mesh axis runs over, the one named last changes fastest.
Arguments:
- residual: float32 [32, 16384], P(None, ('sub', 'blk')), may hold values from -6 to 6
- fine_inverse: float32 [8, 2560, 2048], P('sub', None, 'blk'), may hold values from -1 to 1.1
- coarse_inverse: float32 [2048, 4, 512], P('sub', 'blk'), may hold values from -0.5 to 0.5, as said below
- wanted_rows: int32 [8, 2, 256], P('sub'), may hold values from 0 to 2047
- wanted_count: int32 [8, 2], P('sub'), may hold values from 32 to 256, as said below
- aggregate: int32 [16384], P(('sub', 'blk')), may hold values from 0 to 255
Outputs:
- preconditioned: float32 [32, 16384], P(None, ('sub', 'blk'))
Inputs may be any that keep to these rules, and one draw needn't show every extreme that they name: M of the steps is symmetric: coarse_inverse[i, b, s * 64 + q] equals coarse_inverse[s * 256 + b * 64 + q, b2, s2 * 64 + q2] where i = s2 * 256 + b2 * 64 + q2. `wanted_count`: counts vary from side to side; in every draw some subdomain other than the first and last takes exactly 256 rows from one side.
All inputs are finite; a program needn't handle non-finite values.
Results may differ from a plain program's by a relative error of at most 0.000052.
Values sent between devices are 32-bit elements; how exact they have to be, the bound alone decides.
No kernel may reach another device: no remote copies, remote signals or barrier semaphores. Data moves between devices by JAX's collectives and lax.ppermute only.
A program may use at most 64 MiB of HBM per device.

v0:
```python
import functools

import jax
import jax.numpy as jnp
from jax import lax
from jax.experimental import pallas as pl
from jax.experimental.pallas import tpu as pltpu
from jax.sharding import PartitionSpec as P

BF16 = jnp.bfloat16
F32 = jnp.float32
NN = (((1,), (0,)), ((), ()))
NT = (((1,), (1,)), ((), ()))
LANES = 128
MIB = 1 << 20


def split3(x):
    hi = x.astype(BF16)
    rest = x - hi.astype(F32)
    mid = rest.astype(BF16)
    low = (rest - mid.astype(F32)).astype(BF16)
    return jnp.concatenate([hi, mid, low], axis=0)


def split2(x):
    hi = x.astype(BF16)
    low = (x - hi.astype(F32)).astype(BF16)
    return hi, low


def dot(a, b, dims=NN):
    return lax.dot_general(a, b, dims, preferred_element_type=F32)


def dot3(x, weights):
    rows = x.shape[0]
    x_hi, x_low = split2(x)
    w_hi, w_low = split2(weights)
    both = dot(jnp.concatenate([x_hi, x_low], axis=0), w_hi)
    return both[:rows] + both[rows:] + dot(x_hi, w_low)


def fold3(acc):
    rows = acc.shape[0] // 3
    return acc[:rows] + acc[rows : 2 * rows] + acc[2 * rows :]


def onehot(condition):
    return condition.astype(F32).astype(BF16)


def parity():
    return lax.rem(lax.axis_index("sub"), 2)


def shard_rows(ref, shard, rows, tiles):
    return jnp.concatenate([ref[shard, pl.ds(t * rows, rows)] for t in range(tiles)], axis=1)


def pick(ref, first, rows, tiles, shards, wanted):
    cols = tiles * LANES
    local = lax.broadcasted_iota(jnp.int32, (cols, wanted.shape[1]), 0)
    total = jnp.zeros((3 * rows, wanted.shape[1]), F32)
    for shard in range(shards):
        block = split3(shard_rows(ref, first + shard, rows, tiles))
        total = total + dot(block, onehot(local == wanted - shard * cols))
    return fold3(total)


def pack_kernel(residual_ref, agg_ref, out_ref):
    rows, cols = residual_ref.shape
    tiles = cols // LANES
    codes = [agg_ref[:, t * LANES : (t + 1) * LANES].astype(F32) for t in range(tiles)]
    codes.append(jnp.zeros((out_ref.shape[1] - rows * tiles - tiles, LANES), F32))
    last = jnp.concatenate(codes, axis=0)
    for receiver in range(out_ref.shape[0]):
        for t in range(tiles):
            out_ref[receiver, t * rows : (t + 1) * rows] = residual_ref[:, t * LANES : (t + 1) * LANES]
        out_ref[receiver, rows * tiles :] = last


def coarse_kernel(width, rows, tiles, shards, pair_ref, coarse_ref, fine_ref, send_ref, fine_out, sem):
    fetch = pltpu.make_async_copy(fine_ref, fine_out, sem)
    fetch.start()
    first = parity() * shards
    cols = tiles * LANES
    coarse_len = width * shards
    levels = lax.broadcasted_iota(jnp.int32, (coarse_len, cols), 0)
    rhs = jnp.zeros((3 * rows, coarse_len), F32)
    for shard in range(shards):
        block = split3(shard_rows(pair_ref, first + shard, rows, tiles))
        codes = [pair_ref[first + shard, pl.ds(tiles * rows + t, 1)] for t in range(tiles)]
        unknowns = jnp.concatenate(codes, axis=1).astype(jnp.int32)
        rhs = rhs + dot(block, onehot(levels == unknowns), NT)
    rhs = fold3(rhs)
    half = rows // 2
    lane = lax.broadcasted_iota(jnp.int32, (half, LANES), 1)
    stride = coarse_ref.shape[0] // coarse_len
    step = 2 if stride % 2 == 0 else 1
    for tile in range(0, stride, step):
        parts = [coarse_ref[pl.ds(tile + k, coarse_len, stride=stride), :] for k in range(step)]
        value = dot3(rhs, jnp.concatenate(parts, axis=1))
        for k in range(step):
            part = value[:, k * LANES : (k + 1) * LANES]
            turned = pltpu.roll(part, width, 1)
            left = jnp.where(lane < width, part[:half], turned[half:])
            right = jnp.where(lane < width, turned[:half], part[half:])
            for copy in range(shards):
                send_ref[2 * (tile + k), copy] = left
                send_ref[2 * (tile + k) + 1, copy] = right
    fetch.wait()


def halo_kernel(rows, tiles, shards, pair_ref, lists_ref, out_ref):
    odd = parity()
    wanted = jnp.where(odd == 1, lists_ref[0:1], lists_ref[1:2])
    out_ref[...] = pick(pair_ref, odd * shards, rows, tiles, shards, wanted)


def own_kernel(rows, tiles, shards, counts_ref, pair_ref, lists_ref, fine_ref, out_ref):
    odd = parity()
    cols = tiles * LANES
    margin = lists_ref.shape[1]
    ext = fine_ref.shape[1]
    total = jnp.zeros(out_ref.shape, F32)
    for shard in range(shards):
        block = shard_rows(pair_ref, odd * shards + shard, rows, tiles)
        total = total + dot3(block, fine_ref[0, margin + shard * cols : margin + (shard + 1) * cols])
    slots = lax.broadcasted_iota(jnp.int32, (1, margin), 1)
    wanted = jnp.where(odd == 1, lists_ref[0:1], lists_ref[1:2])
    wanted = jnp.where(slots < counts_ref[0, 1 - odd], wanted, -1)
    halo = pick(pair_ref, (1 - odd) * shards, rows, tiles, shards, wanted)
    start = pl.multiple_of((1 - odd) * (ext - margin), margin)
    out_ref[...] = total + dot3(halo, fine_ref[0, pl.ds(start, margin)])


def tail_kernel(width, counts_ref, got_ref, halo_ref, fine_ref, agg_ref, own_ref, out_ref):
    subs, shards, half, _ = got_ref.shape
    odd = parity()
    margin = halo_ref.shape[1]
    ext = fine_ref.shape[1]
    slots = lax.broadcasted_iota(jnp.int32, halo_ref.shape, 1)
    halo = jnp.where(slots < counts_ref[0, odd], halo_ref[...], 0.0)
    start = pl.multiple_of(odd * (ext - margin), margin)
    total = own_ref[...] + dot3(halo, fine_ref[0, pl.ds(start, margin)])
    sums = [got_ref[0, shard] for shard in range(shards)]
    for sub in range(1, subs):
        for shard in range(shards):
            sums[shard] = sums[shard] + got_ref[sub, shard]
    lane = lax.broadcasted_iota(jnp.int32, (half, LANES), 1)
    top, bottom = [], []
    for pair in range(shards // 2):
        left, right = sums[2 * pair], sums[2 * pair + 1]
        top.append(jnp.where(lane < width, left, pltpu.roll(right, width, 1)))
        bottom.append(jnp.where(lane < width, pltpu.roll(left, width, 1), right))
    coarse = jnp.concatenate([jnp.concatenate(top, axis=1), jnp.concatenate(bottom, axis=1)], axis=0)
    levels = lax.broadcasted_iota(jnp.int32, (coarse.shape[1], out_ref.shape[1]), 0)
    out_ref[...] = total + fold3(dot(split3(coarse), onehot(levels == agg_ref[...])))


def whole(space=pltpu.VMEM):
    return pl.BlockSpec(memory_space=space)


def limit(mib):
    return pltpu.CompilerParams(vmem_limit_bytes=mib * MIB)


def on_device(residual, fine_inverse, coarse_inverse, wanted_rows, wanted_count, aggregate):
    subs = lax.axis_size("sub")
    shards = lax.axis_size("blk")
    rows, cols = residual.shape
    tiles = cols // LANES
    margin = wanted_rows.shape[2]
    coarse_len = coarse_inverse.shape[0]
    width = coarse_len // shards
    group = 2 * shards
    packed_rows = -(-(rows * tiles + tiles) // 8) * 8
    pairs = [list(range(k, k + group)) for k in range(0, subs * shards, group)]
    swaps = [(i, i + 1) for i in range(1, subs - 1, 2)] + [(i + 1, i) for i in range(1, subs - 1, 2)]
    codes = aggregate[None]

    packed = pl.pallas_call(
        pack_kernel,
        out_shape=jax.ShapeDtypeStruct((group, packed_rows, LANES), F32),
        in_specs=[whole(), whole()],
        out_specs=whole(),
        compiler_params=limit(4),
        name="pack",
    )(residual, codes)
    pair = lax.all_to_all(packed, ("sub", "blk"), 0, 0, axis_index_groups=pairs, tiled=True)
    lists = lax.ppermute(wanted_rows[0], "sub", swaps)

    send, fine = pl.pallas_call(
        functools.partial(coarse_kernel, width, rows, tiles, shards),
        out_shape=(
            jax.ShapeDtypeStruct((subs, shards, rows // 2, LANES), F32),
            jax.ShapeDtypeStruct(fine_inverse.shape, F32),
        ),
        in_specs=[whole(), whole(), whole(pl.ANY)],
        out_specs=(whole(), whole()),
        scratch_shapes=[pltpu.SemaphoreType.DMA],
        compiler_params=limit(54),
        name="coarse",
    )(pair, coarse_inverse.reshape(-1, LANES), fine_inverse)
    flat = send.reshape((subs * shards,) + send.shape[2:])
    got = lax.all_to_all(flat, ("sub", "blk"), 0, 0, tiled=True).reshape(send.shape)

    outgoing = pl.pallas_call(
        functools.partial(halo_kernel, rows, tiles, shards),
        out_shape=jax.ShapeDtypeStruct((rows, margin), F32),
        in_specs=[whole(), whole()],
        out_specs=whole(),
        compiler_params=limit(8),
        name="halo",
    )(pair, lists)
    halo = lax.ppermute(outgoing, "sub", swaps)

    owned = pl.pallas_call(
        functools.partial(own_kernel, rows, tiles, shards),
        out_shape=jax.ShapeDtypeStruct((rows, cols), F32),
        in_specs=[whole(pltpu.SMEM), whole(), whole(), whole()],
        out_specs=whole(),
        compiler_params=limit(16),
        cost_estimate=pl.CostEstimate(
            flops=8 * rows * shards * cols * cols,
            bytes_accessed=4 * shards * cols * cols,
            transcendentals=0,
        ),
        name="owned",
    )(wanted_count, pair, wanted_rows[0], fine)

    return pl.pallas_call(
        functools.partial(tail_kernel, width),
        out_shape=jax.ShapeDtypeStruct((rows, cols), F32),
        in_specs=[whole(pltpu.SMEM)] + [whole()] * 5,
        out_specs=whole(),
        compiler_params=limit(16),
        name="tail",
    )(wanted_count, got, halo, fine, codes, owned)


def solution(mesh):
    in_specs = (
        P(None, ("sub", "blk")),
        P("sub", None, "blk"),
        P("sub", "blk", None),
        P("sub", None, None),
        P("sub", None),
        P(("sub", "blk")),
    )
    out_specs = P(None, ("sub", "blk"))
    return jax.shard_map(
        on_device, mesh=mesh, in_specs=in_specs, out_specs=out_specs, check_vma=False
    )
```

profile of v0, /device:TPU:10, one launch (start us, length us, event | category | flops | bytes accessed | tf_op | source)
XLA Modules:
  0.0 45.9 jit_solution(1666329835701373269)
XLA Ops:
  0.0 0.0 copy-start.7
  0.0 0.0 copy-start.3
  0.0 0.9 %copy-done.3 = f32[32,512]{1,0:T(8,128)S(1)} copy-done((f32[32,512]{1,0:T(8,128)S(1)}, f32[32,512]{1,0:T(8,128)}, u32[]{:S(2)}) %copy-start.3) | copy-done | bytes 65560
  0.9 0.0 copy-start.4
  0.9 0.7 %copy-done.4 = s32[512]{0:T(512)S(1)} copy-done((s32[512]{0:T(512)S(1)}, s32[512]{0:T(512)}, u32[]{:S(2)}) %copy-start.4) | copy-done | bytes 2072
  1.5 0.0 copy-start.6
  1.6 12.8 %all_to_all.10.pair_ref = f32[8,136,128]{2,1,0:T(8,128)} all-to-all(f32[8,136,128]{2,1,0:T(8,128)S(1)} %pack.1), channel_id=1, replica_groups={{0,1,2,3,4,5,6,7},{8,9,10,11,12,13,14,15},{16,17,18,19,20,21,22,23},{24..., dimensions={0} | all-to-all | bytes 1114112 | tf_op jit(solution)/shard_map/all_to_all | solution.py:192
  14.4 0.0 copy-start.2
  14.4 0.0 copy-start.5
  14.4 6.1 %coarse.1 = (f32[8,4,16,128]{3,2,1,0:T(8,128)}, f32[1,2560,512]{2,1,0:T(8,128)}) custom-call(f32[8,136,128]{2,1,0:T(8,128)} %all_to_all.10.pair_ref, f32[1024,128]{1,0:T(8,128)} %bitcast.10, f32[1,2560,512]{2,1,0:T(8,128)} %fine_ref.1), custom_call_target="tpu_custom_call" | custom-call | tf_op jit(solution)/shard_map/coarse/pallas_call | solution.py:195
  20.5 5.2 %all-to-all-start.1 = ((f32[32,16,128]{2,1,0:T(8,128)}), f32[32,16,128]{2,1,0:T(8,128)S(1)}, u32[]{:S(2)}, u32[]{:S(2)}) async-start(f32[32,16,128]{2,1,0:T(8,128)} %bitcast.11), calls=%async_computation.1 | async-start | bytes 524288 | tf_op jit(solution)/shard_map/all_to_all | solution.py:208
  25.7 0.0 copy-done.6
  25.7 3.4 %collective-permute-start = (s32[2,256]{1,0:T(2,128)S(1)}, s32[2,256]{1,0:T(2,128)S(1)}, u32[]{:S(2)}, u32[]{:S(2)}) collective-permute-start(s32[2,256]{1,0:T(2,128)S(1)} %bitcast.8), channel_id=1, source_target_pairs={{4,8},{12,16},{20,24},{8,4},{16,12},{24,20},{5,9},{13,17},{21,25},... | collective-permute-start | bytes 6152 | tf_op jit(solution)/shard_map/ppermute | solution.py:193
  29.1 4.8 %collective-permute-done.lists_ref = s32[2,256]{1,0:T(2,128)S(1)} collective-permute-done((s32[2,256]{1,0:T(2,128)S(1)}, s32[2,256]{1,0:T(2,128)S(1)}, u32[]{:S(2)}, u32[]{:S(2)}) %collective-permute-start) | collective-permute-done | bytes 2080 | tf_op jit(solution)/shard_map/ppermute | solution.py:193
  33.9 0.0 copy-done.2
  33.9 0.3 halo.1
  34.2 3.4 %collective-permute-start.1 = (f32[32,256]{1,0:T(8,128)S(1)}, f32[32,256]{1,0:T(8,128)S(1)}, u32[]{:S(2)}, u32[]{:S(2)}) collective-permute-start(f32[32,256]{1,0:T(8,128)S(1)} %halo.1), channel_id=1, source_target_pairs={{4,8},{12,16},{20,24},{8,4},{16,12},{24,20},{5,9},{13,17},{21,25},... | collective-permute-start | bytes 98312 | tf_op jit(solution)/shard_map/ppermute | solution.py:218
  37.6 0.0 copy-done.7
  37.6 0.0 copy-start
  37.7 2.5 %copy-done = f32[1,2560,512]{2,1,0:T(8,128)S(1)} copy-done((f32[1,2560,512]{2,1,0:T(8,128)S(1)}, f32[1,2560,512]{2,1,0:T(8,128)}, u32[]{:S(2)}) %copy-start) | copy-done | bytes 5242904
  40.1 1.8 %owned.1.own_ref = f32[32,512]{1,0:T(8,128)S(1)} custom-call(s32[1,2]{1,0:T(1,128)S(1)} %copy-done.7, f32[8,136,128]{2,1,0:T(8,128)S(1)} %copy-done.2, s32[2,256]{1,0:T(2,128)S(1)} %bitcast.9, f32[1,2560,512]{2,1,0:T(8,128)S(1)} %copy-done), custom_call_target="tpu_custom_call" | custom-call | flops 268435456 | bytes 4194304 | tf_op jit(solution)/shard_map/owned/pallas_call | solution.py:220
  41.9 0.0 collective-permute-done.1.halo_ref
  41.9 0.0 all-to-all-done.1
  42.0 0.0 copy-done.5
  42.0 0.0 copy-start.1
  42.0 2.5 %copy-done.1 = f32[1,2560,512]{2,1,0:T(8,128)S(1)} copy-done((f32[1,2560,512]{2,1,0:T(8,128)S(1)}, f32[1,2560,512]{2,1,0:T(8,128)}, u32[]{:S(2)}) %copy-start.1) | copy-done | bytes 5242904
  44.5 1.5 %tail.1 = f32[32,512]{1,0:T(8,128)} custom-call(s32[1,2]{1,0:T(1,128)S(1)} %copy-done.7, f32[8,4,16,128]{3,2,1,0:T(8,128)S(1)} %bitcast.5, f32[32,256]{1,0:T(8,128)S(1)} %collective-permute-done.1.halo_ref, f32[1,2560,512]{2,1,0:T(8,128)S(1)} %copy-done.1, s32[1,512]{1,0:T(1,128)S(1)} %bitcast.7, f32[32,512]{1,0:T(8,128)S(1)} %owned.1.own_ref), custom_call_target="tpu_custom_call" | custom-call | tf_op jit(solution)/shard_map/tail/pallas_call | solution.py:234
  (1 shorter events, 0.0 us)
Async XLA Ops:
  0.0 37.6 %copy-start.7 = (s32[1,2]{1,0:T(1,128)S(1)}, s32[1,2]{1,0:T(1,128)}, u32[]{:S(2)}) copy-start(s32[1,2]{1,0:T(1,128)} %counts_ref.3) | copy-start | bytes 28
  0.0 0.9 %copy-start.3 = (f32[32,512]{1,0:T(8,128)S(1)}, f32[32,512]{1,0:T(8,128)}, u32[]{:S(2)}) copy-start(f32[32,512]{1,0:T(8,128)} %residual_ref.1) | copy-start | bytes 196612
  0.9 0.7 %copy-start.4 = (s32[512]{0:T(512)S(1)}, s32[512]{0:T(512)}, u32[]{:S(2)}) copy-start(s32[512]{0:T(512)} %param.11) | copy-start | bytes 6148
  1.5 24.2 %copy-start.6 = (s32[1,2,256]{2,1,0:T(2,128)S(1)}, s32[1,2,256]{2,1,0:T(2,128)}, u32[]{:S(2)}) copy-start(s32[1,2,256]{2,1,0:T(2,128)} %param.9) | copy-start | bytes 6148
  14.4 19.5 %copy-start.2 = (f32[8,136,128]{2,1,0:T(8,128)S(1)}, f32[8,136,128]{2,1,0:T(8,128)}, u32[]{:S(2)}) copy-start(f32[8,136,128]{2,1,0:T(8,128)} %all_to_all.10.pair_ref) | copy-start | bytes 1671172
  14.4 27.6 %copy-start.5 = (s32[512]{0:T(512)S(1)}, s32[512]{0:T(512)}, u32[]{:S(2)}) copy-start(s32[512]{0:T(512)} %param.11) | copy-start | bytes 6148
  20.5 21.4 %all-to-all-start.1 = ((f32[32,16,128]{2,1,0:T(8,128)}), f32[32,16,128]{2,1,0:T(8,128)S(1)}, u32[]{:S(2)}, u32[]{:S(2)}) async-start(f32[32,16,128]{2,1,0:T(8,128)} %bitcast.11), calls=%async_computation.1 | async-start | bytes 524288 | tf_op jit(solution)/shard_map/all_to_all | solution.py:208
  25.7 8.2 %collective-permute-start = (s32[2,256]{1,0:T(2,128)S(1)}, s32[2,256]{1,0:T(2,128)S(1)}, u32[]{:S(2)}, u32[]{:S(2)}) collective-permute-start(s32[2,256]{1,0:T(2,128)S(1)} %bitcast.8), channel_id=1, source_target_pairs={{4,8},{12,16},{20,24},{8,4},{16,12},{24,20},{5,9},{13,17},{21,25},... | collective-permute-start | bytes 6152 | tf_op jit(solution)/shard_map/ppermute | solution.py:193
  34.2 7.7 %collective-permute-start.1 = (f32[32,256]{1,0:T(8,128)S(1)}, f32[32,256]{1,0:T(8,128)S(1)}, u32[]{:S(2)}, u32[]{:S(2)}) collective-permute-start(f32[32,256]{1,0:T(8,128)S(1)} %halo.1), channel_id=1, source_target_pairs={{4,8},{12,16},{20,24},{8,4},{16,12},{24,20},{5,9},{13,17},{21,25},... | collective-permute-start | bytes 98312 | tf_op jit(solution)/shard_map/ppermute | solution.py:218
  37.6 2.5 %copy-start = (f32[1,2560,512]{2,1,0:T(8,128)S(1)}, f32[1,2560,512]{2,1,0:T(8,128)}, u32[]{:S(2)}) copy-start(f32[1,2560,512]{2,1,0:T(8,128)} %get-tuple-element.8.fine_ref) | copy-start | bytes 15728644
  42.0 2.5 %copy-start.1 = (f32[1,2560,512]{2,1,0:T(8,128)S(1)}, f32[1,2560,512]{2,1,0:T(8,128)}, u32[]{:S(2)}) copy-start(f32[1,2560,512]{2,1,0:T(8,128)} %get-tuple-element.8.fine_ref) | copy-start | bytes 15728644
where the time goes:
time: 46.3 us; the launch traced here: 45.9 us
  blocking collectives  12.8 us (28%)
  starting transfers between devices  11.9 us (26%)
  Pallas kernels  9.76 us (21%)
  local copies, waits for them, and re-layouts  6.51 us (14%)
  waiting for transfers between devices  4.84 us (10%)
    all_to_all x1, blocking collectives, on_device(): lax.all_to_all(packed, ('sub', 'blk'), 0, 0, axis_index_groups=pairs, til...  12.8 us
    unnamed x16, local copies, waits for them, and re-layouts  6.51 us
    pallas_call x1, Pallas kernels, on_device(): pl.pallas_call(functools.partial(coarse_kernel, width, rows, tiles, shard...  6.15 us
    all_to_all x1, starting transfers between devices, on_device(): lax.all_to_all(flat, ('sub', 'blk'), 0, 0, tiled=True).reshape(send.shape)  5.16 us
    ppermute x1, waiting for transfers between devices, on_device(): lists = lax.ppermute(wanted_rows[0], 'sub', swaps)  4.83 us
    ppermute x1, starting transfers between devices, on_device(): halo = lax.ppermute(outgoing, 'sub', swaps)  3.38 us
    ppermute x1, starting transfers between devices, on_device(): lists = lax.ppermute(wanted_rows[0], 'sub', swaps)  3.37 us
    pallas_call x1, Pallas kernels, on_device(): pl.pallas_call(functools.partial(own_kernel, rows, tiles, shards), out_sh...  1.79 us
  transfers between devices with their start and end apart: 3, of which 1 were waited for; matrix products, arithmetic and copies ran while one was open for 0% of the time, Pallas kernels for 5%

commit v1 on v0

v1 whole, which is shorter than its diff:
```python
import functools

import jax
import jax.numpy as jnp
from jax import lax
from jax.experimental import pallas as pl
from jax.experimental.pallas import tpu as pltpu
from jax.sharding import PartitionSpec as P

BF16 = jnp.bfloat16
F32 = jnp.float32
NN = (((1,), (0,)), ((), ()))
NT = (((1,), (1,)), ((), ()))
LANES = 128
MIB = 1 << 20


def split3(x):
    hi = x.astype(BF16)
    rest = x - hi.astype(F32)
    mid = rest.astype(BF16)
    low = (rest - mid.astype(F32)).astype(BF16)
    return jnp.concatenate([hi, mid, low], axis=0)


def split2(x):
    hi = x.astype(BF16)
    low = (x - hi.astype(F32)).astype(BF16)
    return hi, low


def dot(a, b, dims=NN):
    return lax.dot_general(a, b, dims, preferred_element_type=F32)


def dot_halves(x, w_hi, w_low):
    rows = x.shape[0]
    x_hi, x_low = split2(x)
    both = dot(jnp.concatenate([x_hi, x_low], axis=0), w_hi)
    return both[:rows] + both[rows:] + dot(x_hi, w_low)


def fold3(acc):
    rows = acc.shape[0] // 3
    return acc[:rows] + acc[rows : 2 * rows] + acc[2 * rows :]


def onehot(condition):
    return condition.astype(F32).astype(BF16)


def shard_rows(ref, shard, rows, tiles):
    return jnp.concatenate([ref[shard, pl.ds(t * rows, rows)] for t in range(tiles)], axis=1)


def fold_chunks(part, width):
    half = part.shape[0] // 2
    lane = lax.broadcasted_iota(jnp.int32, (half, LANES), 1)
    turned = pltpu.roll(part, width, 1)
    left = jnp.where(lane < width, part[:half], turned[half:])
    right = jnp.where(lane < width, turned[:half], part[half:])
    return left, right


def unfold_chunks(chunks, width):
    lane = lax.broadcasted_iota(jnp.int32, chunks[0].shape, 1)
    top, bottom = [], []
    for pair in range(len(chunks) // 2):
        left, right = chunks[2 * pair], chunks[2 * pair + 1]
        top.append(jnp.where(lane < width, left, pltpu.roll(right, width, 1)))
        bottom.append(jnp.where(lane < width, pltpu.roll(left, width, 1), right))
    return jnp.concatenate([jnp.concatenate(top, axis=1), jnp.concatenate(bottom, axis=1)], axis=0)


def pack_kernel(residual_ref, agg_ref, lists_ref, out_ref, lists_out, residual_buf, agg_buf, lists_buf, sems):
    fetches = [
        pltpu.make_async_copy(residual_ref, residual_buf, sems.at[0]),
        pltpu.make_async_copy(agg_ref, agg_buf, sems.at[1]),
        pltpu.make_async_copy(lists_ref, lists_buf, sems.at[2]),
    ]
    for fetch in fetches:
        fetch.start()
    for fetch in fetches:
        fetch.wait()
    rows, cols = residual_ref.shape
    tiles = cols // LANES
    codes = [agg_buf[:, t * LANES : (t + 1) * LANES].astype(F32) for t in range(tiles)]
    codes.append(jnp.zeros((out_ref.shape[1] - rows * tiles - tiles, LANES), F32))
    last = jnp.concatenate(codes, axis=0)
    for receiver in range(out_ref.shape[0]):
        for t in range(tiles):
            out_ref[receiver, t * rows : (t + 1) * rows] = residual_buf[:, t * LANES : (t + 1) * LANES]
        out_ref[receiver, rows * tiles :] = last
    for receiver in range(lists_out.shape[0]):
        lists_out[receiver] = lists_buf[...]


def coarse_kernel(width, rows, tiles, own_ref, lists_ref, coarse_ref, send_ref):
    subs = lists_ref.shape[0]
    shards = own_ref.shape[0]
    cols = tiles * LANES
    coarse_len = width * shards
    me, part_id = lax.axis_index("sub"), lax.axis_index("blk")
    per_tile = LANES // width
    last = subs - 1
    above = lists_ref[jnp.minimum(me + 1, last), 0:1]
    below = lists_ref[jnp.maximum(me - 1, 0), 1:2]
    wanted = [above[:, :LANES], below[:, :LANES]]
    for t in range(1, above.shape[1] // LANES):
        here = part_id // per_tile == t
        for side, row in enumerate((above, below)):
            wanted[side] = jnp.where(here, row[:, t * LANES : (t + 1) * LANES], wanted[side])
    wanted = jnp.concatenate(wanted, axis=1)
    levels = lax.broadcasted_iota(jnp.int32, (coarse_len, cols), 0)
    local = lax.broadcasted_iota(jnp.int32, (cols, 2 * LANES), 0)
    rhs = jnp.zeros((3 * rows, coarse_len), F32)
    picked = jnp.zeros((3 * rows, 2 * LANES), F32)
    for shard in range(shards):
        block = split3(shard_rows(own_ref, shard, rows, tiles))
        codes = [own_ref[shard, pl.ds(tiles * rows + t, 1)] for t in range(tiles)]
        unknowns = jnp.concatenate(codes, axis=1).astype(jnp.int32)
        rhs = rhs + dot(block, onehot(levels == unknowns), NT)
        picked = picked + dot(block, onehot(local == wanted - shard * cols))
    rhs, picked = fold3(rhs), fold3(picked)
    half = rows // 2
    quarters = []
    for side in range(2):
        left, right = fold_chunks(picked[:, side * LANES : (side + 1) * LANES], width)
        quarters.append(jnp.where(lax.rem(part_id, per_tile) == 0, left, right))
    stride = coarse_ref.shape[0] // coarse_len
    for tile in range(0, stride, 2):
        parts = [coarse_ref[pl.ds(tile + k, coarse_len, stride=stride), :] for k in range(2)]
        value = dot_halves(rhs, *split2(jnp.concatenate(parts, axis=1)))
        for k in range(2):
            chunks = fold_chunks(value[:, k * LANES : (k + 1) * LANES], width)
            for e in range(2):
                to = 2 * (tile + k) + e
                send_ref[to, :half] = chunks[e]
                margin = jnp.where(me + 1 == to, quarters[0], jnp.where(me == to + 1, quarters[1], 0.0))
                send_ref[to, half:] = margin


def own_kernel(
    rows, tiles, margin, own_ref, agg_ref, fine_ref, out_ref, hi_ref, low_ref, hot_ref, fine_buf, sems
):
    shards = own_ref.shape[0]
    cols = tiles * LANES
    ext = fine_ref.shape[1]
    pieces = [(margin + shard * cols, cols) for shard in range(shards)]
    pieces += [(0, margin), (ext - margin, margin)]
    copies = []
    for k, (start, size) in enumerate(pieces):
        copies.append(
            pltpu.make_async_copy(
                fine_ref.at[0, pl.ds(start, size)], fine_buf.at[pl.ds(start, size)], sems.at[k]
            )
        )
        copies[k].start()
    levels = lax.broadcasted_iota(jnp.int32, hot_ref.shape, 0)
    hot_ref[...] = onehot(levels == agg_ref[...])
    total = jnp.zeros(out_ref.shape, F32)
    for shard in range(shards):
        start = pieces[shard][0]
        copies[shard].wait()
        block = shard_rows(own_ref, shard, rows, tiles)
        total = total + dot_halves(block, *split2(fine_buf[start : start + cols]))
    out_ref[...] = total
    for side in range(2):
        start = pieces[shards + side][0]
        copies[shards + side].wait()
        hi_ref[side], low_ref[side] = split2(fine_buf[start : start + margin])


def reduce_kernel(got_ref, out_ref):
    subs = got_ref.shape[0]
    half = got_ref.shape[1] // 2
    me = lax.axis_index("sub")
    last = subs - 1
    total = got_ref[0, :half]
    for sub in range(1, subs):
        total = total + got_ref[sub, :half]
    left = jnp.where(me > 0, got_ref[jnp.maximum(me - 1, 0), half:], 0.0)
    right = jnp.where(me < last, got_ref[jnp.minimum(me + 1, last), half:], 0.0)
    for receiver in range(out_ref.shape[0]):
        out_ref[receiver, :half] = total
        out_ref[receiver, half : 2 * half] = left
        out_ref[receiver, 2 * half :] = right


def tail_kernel(width, counts_ref, got_ref, hi_ref, low_ref, hot_ref, own_ref, out_ref):
    shards = got_ref.shape[0]
    half = got_ref.shape[1] // 3
    coarse = unfold_chunks([got_ref[k, :half] for k in range(shards)], width)
    total = own_ref[...] + fold3(dot(split3(coarse), hot_ref[...]))
    for side in range(2):
        first = (1 + side) * half
        halo = unfold_chunks([got_ref[k, first : first + half] for k in range(shards)], width)
        slots = lax.broadcasted_iota(jnp.int32, halo.shape, 1)
        halo = jnp.where(slots < counts_ref[0, side], halo, 0.0)
        total = total + dot_halves(halo, hi_ref[side], low_ref[side])
    out_ref[...] = total


def whole(space=pltpu.VMEM):
    return pl.BlockSpec(memory_space=space)


def limit(mib):
    return pltpu.CompilerParams(vmem_limit_bytes=mib * MIB)


def on_device(residual, fine_inverse, coarse_inverse, wanted_rows, wanted_count, aggregate):
    subs = lax.axis_size("sub")
    shards = lax.axis_size("blk")
    rows, cols = residual.shape
    tiles = cols // LANES
    sides, margin = wanted_rows.shape[1:]
    coarse_len = coarse_inverse.shape[0]
    width = coarse_len // shards
    half = rows // 2
    packed_rows = -(-(rows * tiles + tiles) // 8) * 8
    codes = aggregate[None]

    packed, lists = pl.pallas_call(
        pack_kernel,
        out_shape=(
            jax.ShapeDtypeStruct((shards, packed_rows, LANES), F32),
            jax.ShapeDtypeStruct((subs, sides, margin), jnp.int32),
        ),
        in_specs=[whole(pl.ANY)] * 3,
        out_specs=(whole(), whole()),
        scratch_shapes=[
            pltpu.VMEM(residual.shape, F32),
            pltpu.VMEM(codes.shape, jnp.int32),
            pltpu.VMEM(wanted_rows.shape[1:], jnp.int32),
            pltpu.SemaphoreType.DMA((3,)),
        ],
        compiler_params=limit(60),
        name="pack",
    )(residual, codes, wanted_rows[0])
    own = lax.all_to_all(packed, "blk", 0, 0, tiled=True)
    lists = lax.all_to_all(lists, "sub", 0, 0, tiled=True)

    send = pl.pallas_call(
        functools.partial(coarse_kernel, width, rows, tiles),
        out_shape=jax.ShapeDtypeStruct((subs, 2 * half, LANES), F32),
        in_specs=[whole()] * 3,
        out_specs=whole(),
        compiler_params=limit(12),
        name="coarse",
    )(own, lists, coarse_inverse.reshape(-1, LANES))
    got = lax.all_to_all(send, "sub", 0, 0, tiled=True)

    owned, w_hi, w_low, hot = pl.pallas_call(
        functools.partial(own_kernel, rows, tiles, margin),
        out_shape=(
            jax.ShapeDtypeStruct((rows, cols), F32),
            jax.ShapeDtypeStruct((2, margin, cols), BF16),
            jax.ShapeDtypeStruct((2, margin, cols), BF16),
            jax.ShapeDtypeStruct((coarse_len, cols), BF16),
        ),
        in_specs=[whole(), whole(), whole(pl.ANY)],
        out_specs=(whole(),) * 4,
        scratch_shapes=[
            pltpu.VMEM(fine_inverse.shape[1:], F32),
            pltpu.SemaphoreType.DMA((shards + 2,)),
        ],
        compiler_params=limit(48),
        cost_estimate=pl.CostEstimate(
            flops=6 * rows * shards * cols * cols,
            bytes_accessed=4 * (shards * cols + 2 * margin) * cols,
            transcendentals=0,
        ),
        name="owned",
    )(own, codes, fine_inverse)

    shared = pl.pallas_call(
        reduce_kernel,
        out_shape=jax.ShapeDtypeStruct((shards, 3 * half, LANES), F32),
        in_specs=[whole()],
        out_specs=whole(),
        compiler_params=limit(8),
        name="reduce",
    )(got)
    parts = lax.all_to_all(shared, "blk", 0, 0, tiled=True)

    return pl.pallas_call(
        functools.partial(tail_kernel, width),
        out_shape=jax.ShapeDtypeStruct((rows, cols), F32),
        in_specs=[whole(pltpu.SMEM)] + [whole()] * 5,
        out_specs=whole(),
        compiler_params=limit(12),
        name="tail",
    )(wanted_count, parts, w_hi, w_low, hot, owned)


def solution(mesh):
    in_specs = (
        P(None, ("sub", "blk")),
        P("sub", None, "blk"),
        P("sub", "blk", None),
        P("sub", None, None),
        P("sub", None),
        P(("sub", "blk")),
    )
    out_specs = P(None, ("sub", "blk"))
    return jax.shard_map(
        on_device, mesh=mesh, in_specs=in_specs, out_specs=out_specs, check_vma=False
    )
```

time: 46.3 us -> 47.2 us (1.019)
  the two profiles are of different devices: /device:TPU:10 before, /device:TPU:0 now
where the time goes in v1:
time: 47.2 us; the launch traced here: 46.7 us
  blocking collectives  33.3 us (71%)
  Pallas kernels  7.45 us (16%)
  starting transfers between devices  3.3 us (7%)
  local copies, waits for them, and re-layouts  1.72 us (4%)
  waiting for transfers between devices  0.87 us (2%)
    all_to_all x1, blocking collectives, on_device(): lists = lax.all_to_all(lists, 'sub', 0, 0, tiled=True)  13.8 us
    all_to_all x1, blocking collectives, on_device(): got = lax.all_to_all(send, 'sub', 0, 0, tiled=True)  9.86 us
    all_to_all x1, blocking collectives, on_device(): own = lax.all_to_all(packed, 'blk', 0, 0, tiled=True)  9.63 us
    all_to_all x1, starting transfers between devices, on_device(): parts = lax.all_to_all(shared, 'blk', 0, 0, tiled=True)  3.3 us
    pallas_call x1, Pallas kernels, on_device(): pl.pallas_call(functools.partial(own_kernel, rows, tiles, margin), out_sh...  2.7 us
    unnamed x6, local copies, waits for them, and re-layouts  1.72 us
    pallas_call x1, Pallas kernels, on_device(): pl.pallas_call(pack_kernel, out_shape=(jax.ShapeDtypeStruct((shards, pack...  1.61 us
    pallas_call x1, Pallas kernels, on_device(): pl.pallas_call(functools.partial(tail_kernel, width), out_shape=jax.Shape...  1.54 us
  transfers between devices with their start and end apart: 1, of which 1 were waited for; matrix products, arithmetic and copies ran while one was open for 0% of the time, Pallas kernels for 6%

profile of v1, /device:TPU:0, one launch (start us, length us, event | category | flops | bytes accessed | tf_op | source)
XLA Modules:
  0.0 46.7 jit_solution(2097827065926310485)
XLA Ops:
  0.0 0.0 copy-start.2
  0.0 1.6 %pack.1 = (f32[4,136,128]{2,1,0:T(8,128)}, s32[8,2,256]{2,1,0:T(2,128)}) custom-call(f32[32,512]{1,0:T(8,128)} %residual_ref.1, s32[1,512]{1,0:T(1,128)} %bitcast.4, s32[2,256]{1,0:T(2,128)} %bitcast.6), custom_call_target="tpu_custom_call" | custom-call | tf_op jit(solution)/shard_map/pack/pallas_call | solution.py:224
  1.6 13.8 %all_to_all.20.lists_ref = s32[8,2,256]{2,1,0:T(2,128)S(1)} all-to-all(s32[8,2,256]{2,1,0:T(2,128)} %get-tuple-element.12), channel_id=1, replica_groups=mesh['sub'=8,'blk'=4] {'sub'}, dimensions={0} | all-to-all | bytes 32768 | tf_op jit(solution)/shard_map/all_to_all | solution.py:242
  15.5 9.6 %all_to_all.21.own_ref = f32[4,136,128]{2,1,0:T(8,128)S(1)} all-to-all(f32[4,136,128]{2,1,0:T(8,128)} %get-tuple-element.11), channel_id=1, replica_groups=mesh['sub'=8,'blk'=4] {'blk'}, dimensions={0} | all-to-all | bytes 557056 | tf_op jit(solution)/shard_map/all_to_all | solution.py:241
  25.1 0.0 copy-start
  25.1 1.0 %copy-done = f32[256,1,512]{2,1,0:T(1,128)S(1)} copy-done((f32[256,1,512]{2,1,0:T(1,128)S(1)}, f32[256,1,512]{2,1,0:T(1,128)}, u32[]{:S(2)}) %copy-start) | copy-done | bytes 524312
  26.1 0.9 %coarse.1 = f32[8,32,128]{2,1,0:T(8,128)S(1)} custom-call(f32[4,136,128]{2,1,0:T(8,128)S(1)} %all_to_all.21.own_ref, s32[8,2,256]{2,1,0:T(2,128)S(1)} %all_to_all.20.lists_ref, f32[1024,128]{1,0:T(8,128)S(1)} %bitcast.3), custom_call_target="tpu_custom_call" | custom-call | tf_op jit(solution)/shard_map/coarse/pallas_call | solution.py:244
  27.1 9.9 %all_to_all.22.got_ref = f32[8,32,128]{2,1,0:T(8,128)S(1)} all-to-all(f32[8,32,128]{2,1,0:T(8,128)S(1)} %coarse.1), channel_id=1, replica_groups=mesh['sub'=8,'blk'=4] {'sub'}, dimensions={0} | all-to-all | bytes 262144 | tf_op jit(solution)/shard_map/all_to_all | solution.py:252
  36.9 0.7 %reduce.1 = f32[4,48,128]{2,1,0:T(8,128)} custom-call(f32[8,32,128]{2,1,0:T(8,128)S(1)} %all_to_all.22.got_ref), custom_call_target="tpu_custom_call" | custom-call | tf_op jit(solution)/shard_map/reduce/pallas_call | solution.py:277
  37.6 3.3 %all-to-all-start.3 = ((f32[4,48,128]{2,1,0:T(8,128)}), f32[4,48,128]{2,1,0:T(8,128)S(1)}, u32[]{:S(2)}, u32[]{:S(2)}) async-start(f32[4,48,128]{2,1,0:T(8,128)} %reduce.1), calls=%async_computation.3 | async-start | bytes 196608 | tf_op jit(solution)/shard_map/all_to_all | solution.py:285
  40.9 0.0 copy-start.1
  40.9 0.7 %copy-done.1 = s32[512]{0:T(512)S(1)} copy-done((s32[512]{0:T(512)S(1)}, s32[512]{0:T(512)}, u32[]{:S(2)}) %copy-start.1) | copy-done | bytes 2072
  41.6 2.7 %owned.1 = (f32[32,512]{1,0:T(8,128)S(1)}, bf16[2,256,512]{2,1,0:T(8,128)(2,1)S(1)}, bf16[2,256,512]{2,1,0:T(8,128)(2,1)S(1)}, bf16[256,512]{1,0:T(8,128)(2,1)S(1)}) custom-call(f32[4,136,128]{2,1,0:T(8,128)S(1)} %all_to_all.21.own_ref, s32[1,512]{1,0:T(1,128)S(1)} %bitcast.5, f32[1,2560,512]{2,1,0:T(8,128)} %fine_ref.1), custom_call_target="tpu_custom_call" | custom-call | flops 201326592 | bytes 5242880 | tf_op jit(solution)/shard_map/owned/pallas_call | solution.py:254
  44.3 0.9 %all-to-all-done.3.got_ref = f32[4,48,128]{2,1,0:T(8,128)S(1)} async-done(((f32[4,48,128]{2,1,0:T(8,128)}), f32[4,48,128]{2,1,0:T(8,128)S(1)}, u32[]{:S(2)}, u32[]{:S(2)}) %all-to-all-start.3) | async-done | bytes 98336 | tf_op jit(solution)/shard_map/all_to_all | solution.py:285
  45.2 0.0 copy-done.2
  45.2 1.5 %tail.1 = f32[32,512]{1,0:T(8,128)} custom-call(s32[1,2]{1,0:T(1,128)S(1)} %copy-done.2, f32[4,48,128]{2,1,0:T(8,128)S(1)} %all-to-all-done.3.got_ref, bf16[2,256,512]{2,1,0:T(8,128)(2,1)S(1)} %get-tuple-element.13.hi_ref, bf16[2,256,512]{2,1,0:T(8,128)(2,1)S(1)} %get-tuple-element.14.low_ref, bf16[256,512]{1,0:T(8,128)(2,1)S(1)} %get-tuple-element.15.hot_ref, ...), custom_call_target="tpu_custom_call" | custom-call | tf_op jit(solution)/shard_map/tail/pallas_call | solution.py:287
Async XLA Ops:
  0.0 45.2 %copy-start.2 = (s32[1,2]{1,0:T(1,128)S(1)}, s32[1,2]{1,0:T(1,128)}, u32[]{:S(2)}) copy-start(s32[1,2]{1,0:T(1,128)} %counts_ref.1) | copy-start | bytes 28
  25.1 1.0 %copy-start = (f32[256,1,512]{2,1,0:T(1,128)S(1)}, f32[256,1,512]{2,1,0:T(1,128)}, u32[]{:S(2)}) copy-start(f32[256,1,512]{2,1,0:T(1,128)} %param.8) | copy-start | bytes 1572868
  37.6 7.6 %all-to-all-start.3 = ((f32[4,48,128]{2,1,0:T(8,128)}), f32[4,48,128]{2,1,0:T(8,128)S(1)}, u32[]{:S(2)}, u32[]{:S(2)}) async-start(f32[4,48,128]{2,1,0:T(8,128)} %reduce.1), calls=%async_computation.3 | async-start | bytes 196608 | tf_op jit(solution)/shard_map/all_to_all | solution.py:285
  40.9 0.7 %copy-start.1 = (s32[512]{0:T(512)S(1)}, s32[512]{0:T(512)}, u32[]{:S(2)}) copy-start(s32[512]{0:T(512)} %param.11) | copy-start | bytes 6148

commit v2 on v1

v2 whole, which is shorter than its diff:
```python
import functools

import jax
import jax.numpy as jnp
from jax import lax
from jax.experimental import pallas as pl
from jax.experimental.pallas import tpu as pltpu
from jax.sharding import PartitionSpec as P

BF16 = jnp.bfloat16
F32 = jnp.float32
NN = (((1,), (0,)), ((), ()))
NT = (((1,), (1,)), ((), ()))
LANES = 128
MIB = 1 << 20


def split3(x):
    hi = x.astype(BF16)
    rest = x - hi.astype(F32)
    mid = rest.astype(BF16)
    low = (rest - mid.astype(F32)).astype(BF16)
    return jnp.concatenate([hi, mid, low], axis=0)


def split2(x):
    hi = x.astype(BF16)
    low = (x - hi.astype(F32)).astype(BF16)
    return hi, low


def dot(a, b, dims=NN):
    return lax.dot_general(a, b, dims, preferred_element_type=F32)


def dot_halves(x, w_hi, w_low):
    rows = x.shape[0]
    x_hi, x_low = split2(x)
    both = dot(jnp.concatenate([x_hi, x_low], axis=0), w_hi)
    return both[:rows] + both[rows:] + dot(x_hi, w_low)


def fold3(acc):
    rows = acc.shape[0] // 3
    return acc[:rows] + acc[rows : 2 * rows] + acc[2 * rows :]


def onehot(condition):
    return condition.astype(F32).astype(BF16)


def shard_rows(ref, shard, rows, tiles):
    return jnp.concatenate([ref[shard, pl.ds(t * rows, rows)] for t in range(tiles)], axis=1)


def pick(ref, rows, tiles, wanted):
    cols = tiles * LANES
    local = lax.broadcasted_iota(jnp.int32, (cols, wanted.shape[1]), 0)
    total = jnp.zeros((3 * rows, wanted.shape[1]), F32)
    for shard in range(ref.shape[0]):
        block = split3(shard_rows(ref, shard, rows, tiles))
        total = total + dot(block, onehot(local == wanted - shard * cols))
    return fold3(total)


def parity():
    return lax.rem(lax.axis_index("sub"), 2)


def pack_kernel(residual_ref, agg_ref, coarse_ref, out_ref, coarse_out, residual_buf, agg_buf, sems):
    fetches = [
        pltpu.make_async_copy(residual_ref, residual_buf, sems.at[0]),
        pltpu.make_async_copy(agg_ref, agg_buf, sems.at[1]),
        pltpu.make_async_copy(coarse_ref, coarse_out, sems.at[2]),
    ]
    for fetch in fetches:
        fetch.start()
    fetches[0].wait()
    fetches[1].wait()
    rows, cols = residual_buf.shape
    tiles = cols // LANES
    codes = [agg_buf[:, t * LANES : (t + 1) * LANES].astype(F32) for t in range(tiles)]
    codes.append(jnp.zeros((out_ref.shape[1] - rows * tiles - tiles, LANES), F32))
    last = jnp.concatenate(codes, axis=0)
    for receiver in range(out_ref.shape[0]):
        for t in range(tiles):
            out_ref[receiver, t * rows : (t + 1) * rows] = residual_buf[:, t * LANES : (t + 1) * LANES]
        out_ref[receiver, rows * tiles :] = last
    fetches[2].wait()


def coarse_kernel(width, rows, tiles, own_ref, coarse_ref, send_ref):
    shards = own_ref.shape[0]
    cols = tiles * LANES
    coarse_len = width * shards
    levels = lax.broadcasted_iota(jnp.int32, (coarse_len, cols), 0)
    rhs = jnp.zeros((3 * rows, coarse_len), F32)
    for shard in range(shards):
        block = split3(shard_rows(own_ref, shard, rows, tiles))
        codes = [own_ref[shard, pl.ds(tiles * rows + t, 1)] for t in range(tiles)]
        unknowns = jnp.concatenate(codes, axis=1).astype(jnp.int32)
        rhs = rhs + dot(block, onehot(levels == unknowns), NT)
    rhs = fold3(rhs)
    half = rows // 2
    lane = lax.broadcasted_iota(jnp.int32, (half, LANES), 1)
    stride = coarse_ref.shape[0] // coarse_len
    for tile in range(0, stride, 2):
        parts = [coarse_ref[pl.ds(tile + k, coarse_len, stride=stride), :] for k in range(2)]
        value = dot_halves(rhs, *split2(jnp.concatenate(parts, axis=1)))
        for k in range(2):
            part = value[:, k * LANES : (k + 1) * LANES]
            turned = pltpu.roll(part, width, 1)
            left = jnp.where(lane < width, part[:half], turned[half:])
            right = jnp.where(lane < width, turned[:half], part[half:])
            for copy in range(shards):
                send_ref[2 * (tile + k), copy] = left
                send_ref[2 * (tile + k) + 1, copy] = right


def outer_kernel(rows, tiles, own_ref, lists_ref, out_ref):
    wanted = jnp.where(parity() == 1, lists_ref[0:1], lists_ref[1:2])
    out_ref[...] = pick(own_ref, rows, tiles, wanted)


def own_kernel(
    rows, tiles, margin, own_ref, agg_ref, fine_ref, out_ref, hi_ref, low_ref, hot_ref, fine_buf, agg_buf, sems
):
    shards = own_ref.shape[0]
    cols = tiles * LANES
    ext = fine_ref.shape[1]
    pieces = [(margin + shard * cols, cols) for shard in range(shards)]
    pieces += [(0, margin), (ext - margin, margin)]
    copies = []
    for k, (start, size) in enumerate(pieces):
        copies.append(
            pltpu.make_async_copy(
                fine_ref.at[0, pl.ds(start, size)], fine_buf.at[pl.ds(start, size)], sems.at[k]
            )
        )
        copies[k].start()
    fetch = pltpu.make_async_copy(agg_ref, agg_buf, sems.at[shards + 2])
    fetch.start()
    fetch.wait()
    levels = lax.broadcasted_iota(jnp.int32, hot_ref.shape, 0)
    hot_ref[...] = onehot(levels == agg_buf[...])
    total = jnp.zeros(out_ref.shape, F32)
    for shard in range(shards):
        start = pieces[shard][0]
        copies[shard].wait()
        block = shard_rows(own_ref, shard, rows, tiles)
        total = total + dot_halves(block, *split2(fine_buf[start : start + cols]))
    out_ref[...] = total
    for side in range(2):
        start = pieces[shards + side][0]
        copies[shards + side].wait()
        hi_ref[side], low_ref[side] = split2(fine_buf[start : start + margin])


def inner_kernel(rows, tiles, counts_ref, other_ref, lists_ref, hi_ref, low_ref, total_ref, out_ref):
    odd = parity()
    slots = lax.broadcasted_iota(jnp.int32, (1, lists_ref.shape[1]), 1)
    wanted = jnp.where(odd == 1, lists_ref[0:1], lists_ref[1:2])
    wanted = jnp.where(slots < counts_ref[0, 1 - odd], wanted, -1)
    halo = pick(other_ref, rows, tiles, wanted)
    out_ref[...] = total_ref[...] + dot_halves(halo, hi_ref[1 - odd], low_ref[1 - odd])


def tail_kernel(width, counts_ref, got_ref, halo_ref, hi_ref, low_ref, hot_ref, total_ref, out_ref):
    subs, shards, half, _ = got_ref.shape
    odd = parity()
    slots = lax.broadcasted_iota(jnp.int32, halo_ref.shape, 1)
    halo = jnp.where(slots < counts_ref[0, odd], halo_ref[...], 0.0)
    total = total_ref[...] + dot_halves(halo, hi_ref[odd], low_ref[odd])
    sums = [got_ref[0, shard] for shard in range(shards)]
    for sub in range(1, subs):
        for shard in range(shards):
            sums[shard] = sums[shard] + got_ref[sub, shard]
    lane = lax.broadcasted_iota(jnp.int32, (half, LANES), 1)
    top, bottom = [], []
    for pair in range(shards // 2):
        left, right = sums[2 * pair], sums[2 * pair + 1]
        top.append(jnp.where(lane < width, left, pltpu.roll(right, width, 1)))
        bottom.append(jnp.where(lane < width, pltpu.roll(left, width, 1), right))
    coarse = jnp.concatenate([jnp.concatenate(top, axis=1), jnp.concatenate(bottom, axis=1)], axis=0)
    out_ref[...] = total + fold3(dot(split3(coarse), hot_ref[...]))


def whole(space=pltpu.VMEM):
    return pl.BlockSpec(memory_space=space)


def limit(mib):
    return pltpu.CompilerParams(vmem_limit_bytes=mib * MIB)


def in_hbm(x):
    return pltpu.with_memory_space_constraint(x, pltpu.HBM)


def weight(flops):
    return pl.CostEstimate(flops=flops, bytes_accessed=0, transcendentals=0)


def on_device(residual, fine_inverse, coarse_inverse, wanted_rows, wanted_count, aggregate):
    subs = lax.axis_size("sub")
    shards = lax.axis_size("blk")
    rows, cols = residual.shape
    tiles = cols // LANES
    margin = wanted_rows.shape[2]
    coarse_len = coarse_inverse.shape[0]
    width = coarse_len // shards
    packed_rows = -(-(rows * tiles + tiles) // 8) * 8
    inner = [(i, i + 1) for i in range(0, subs, 2)] + [(i + 1, i) for i in range(0, subs, 2)]
    outer = [(i, i + 1) for i in range(1, subs - 1, 2)] + [(i + 1, i) for i in range(1, subs - 1, 2)]
    codes = in_hbm(aggregate[None])
    table = coarse_inverse.reshape(-1, LANES)

    packed, table = pl.pallas_call(
        pack_kernel,
        out_shape=(
            jax.ShapeDtypeStruct((shards, packed_rows, LANES), F32),
            jax.ShapeDtypeStruct(table.shape, F32),
        ),
        in_specs=[whole(pl.ANY)] * 3,
        out_specs=(whole(), whole()),
        scratch_shapes=[
            pltpu.VMEM(residual.shape, F32),
            pltpu.VMEM(codes.shape, jnp.int32),
            pltpu.SemaphoreType.DMA((3,)),
        ],
        compiler_params=limit(4),
        name="pack",
    )(in_hbm(residual), codes, in_hbm(table))
    own = lax.all_to_all(packed, "blk", 0, 0, tiled=True)
    lists = lax.ppermute(wanted_rows[0], "sub", outer)

    send = pl.pallas_call(
        functools.partial(coarse_kernel, width, rows, tiles),
        out_shape=jax.ShapeDtypeStruct((subs, shards, rows // 2, LANES), F32),
        in_specs=[whole()] * 2,
        out_specs=whole(),
        compiler_params=limit(12),
        cost_estimate=weight(8 * 10**9),
        name="coarse",
    )(own, table)
    flat = send.reshape((subs * shards,) + send.shape[2:])
    got = lax.all_to_all(flat, ("sub", "blk"), 0, 0, tiled=True).reshape(send.shape)

    outgoing = pl.pallas_call(
        functools.partial(outer_kernel, rows, tiles),
        out_shape=jax.ShapeDtypeStruct((rows, margin), F32),
        in_specs=[whole(), whole()],
        out_specs=whole(),
        compiler_params=limit(8),
        name="outer",
    )(own, lists)
    halo = lax.ppermute(outgoing, "sub", outer)
    other = lax.ppermute(own, "sub", inner)

    owned, w_hi, w_low, hot = pl.pallas_call(
        functools.partial(own_kernel, rows, tiles, margin),
        out_shape=(
            jax.ShapeDtypeStruct((rows, cols), F32),
            jax.ShapeDtypeStruct((2, margin, cols), BF16),
            jax.ShapeDtypeStruct((2, margin, cols), BF16),
            jax.ShapeDtypeStruct((coarse_len, cols), BF16),
        ),
        in_specs=[whole(), whole(pl.ANY), whole(pl.ANY)],
        out_specs=(whole(),) * 4,
        scratch_shapes=[
            pltpu.VMEM(fine_inverse.shape[1:], F32),
            pltpu.VMEM(codes.shape, jnp.int32),
            pltpu.SemaphoreType.DMA((shards + 3,)),
        ],
        compiler_params=limit(16),
        cost_estimate=weight(40 * 10**9),
        name="owned",
    )(own, codes, in_hbm(fine_inverse))

    fine = pl.pallas_call(
        functools.partial(inner_kernel, rows, tiles),
        out_shape=jax.ShapeDtypeStruct((rows, cols), F32),
        in_specs=[whole(pltpu.SMEM)] + [whole()] * 5,
        out_specs=whole(),
        compiler_params=limit(8),
        name="inner",
    )(wanted_count, other, wanted_rows[0], w_hi, w_low, owned)

    return pl.pallas_call(
        functools.partial(tail_kernel, width),
        out_shape=jax.ShapeDtypeStruct((rows, cols), F32),
        in_specs=[whole(pltpu.SMEM)] + [whole()] * 6,
        out_specs=whole(),
        compiler_params=limit(12),
        name="tail",
    )(wanted_count, got, halo, w_hi, w_low, hot, fine)


def solution(mesh):
    in_specs = (
        P(None, ("sub", "blk")),
        P("sub", None, "blk"),
        P("sub", "blk", None),
        P("sub", None, None),
        P("sub", None),
        P(("sub", "blk")),
    )
    out_specs = P(None, ("sub", "blk"))
    return jax.shard_map(
        on_device, mesh=mesh, in_specs=in_specs, out_specs=out_specs, check_vma=False
    )
```

time: 47.2 us -> 35.7 us (0.76)
  blocking collectives: 33.3 us -> 0 us
  starting transfers between devices: 3.3 us -> 15.8 us
  waiting for transfers between devices: 0.87 us -> 9.76 us
  Pallas kernels: 7.45 us -> 9.71 us
  local copies, waits for them, and re-layouts: 1.72 us -> 0.03 us
    all_to_all x3 -> x0, blocking collectives: 33.3 us -> none  [the longest x1 13.8 us: on_device(): lists = lax.all_to_all(lists, 'sub', 0, 0, tiled=True)]
    all_to_all x1 -> x2, starting transfers between devices: 3.3 us -> 9.77 us  [the longest x1 5.53 us: on_device(): lax.all_to_all(flat, ('sub', 'blk'), 0, 0, tiled=True).reshape(send.shape)]
    ppermute x0 -> x3, starting transfers between devices: none -> 5.99 us  [the longest x1 4.54 us: on_device(): other = lax.ppermute(own, 'sub', inner)]
    all_to_all x1 -> x2, waiting for transfers between devices: 0.87 us -> 5.56 us  [the longest x1 5.56 us: on_device(): own = lax.all_to_all(packed, 'blk', 0, 0, tiled=True)]
    ppermute x0 -> x3, waiting for transfers between devices: none -> 4.21 us  [the longest x1 4.19 us: on_device(): other = lax.ppermute(own, 'sub', inner)]
    unnamed x6 -> x4, local copies, waits for them, and re-layouts: 1.72 us -> 0.03 us
    pallas_call x1 -> x2, Pallas kernels: 0.65 us -> 1.47 us  [the longest x1 1.14 us: on_device(): pl.pallas_call(functools.partial(inner_kernel, rows, tiles), out_shape=ja...]
    pallas_call x1, Pallas kernels: 2.7 us -> 3.43 us  [on_device(): pl.pallas_call(functools.partial(own_kernel, rows, tiles, margin), out_sh...]
  transfers between devices with their start and end apart: 1 -> 5, of which waited for: 1 -> 2; matrix products, arithmetic and copies ran while one was open for 0% -> 0% of each run, Pallas kernels for 6% -> 18%
where the time goes in v2:
time: 35.7 us; the launch traced here: 35.4 us
  starting transfers between devices  15.8 us (44%)
  waiting for transfers between devices  9.76 us (27%)
  Pallas kernels  9.71 us (27%)
    all_to_all x1, waiting for transfers between devices, on_device(): own = lax.all_to_all(packed, 'blk', 0, 0, tiled=True)  5.56 us
    all_to_all x1, starting transfers between devices, on_device(): lax.all_to_all(flat, ('sub', 'blk'), 0, 0, tiled=True).reshape(send.shape)  5.53 us
    ppermute x1, starting transfers between devices, on_device(): other = lax.ppermute(own, 'sub', inner)  4.54 us
    all_to_all x1, starting transfers between devices, on_device(): own = lax.all_to_all(packed, 'blk', 0, 0, tiled=True)  4.25 us
    ppermute x1, waiting for transfers between devices, on_device(): other = lax.ppermute(own, 'sub', inner)  4.19 us
    pallas_call x1, Pallas kernels, on_device(): pl.pallas_call(functools.partial(own_kernel, rows, tiles, margin), out_sh...  3.43 us
    pallas_call x1, Pallas kernels, on_device(): pl.pallas_call(pack_kernel, out_shape=(jax.ShapeDtypeStruct((shards, pack...  1.83 us
    pallas_call x1, Pallas kernels, on_device(): pl.pallas_call(functools.partial(coarse_kernel, width, rows, tiles), out_...  1.54 us
  transfers between devices with their start and end apart: 5, of which 2 were waited for; matrix products, arithmetic and copies ran while one was open for 0% of the time, Pallas kernels for 18%

profile of v2, /device:TPU:0, one launch (start us, length us, event | category | flops | bytes accessed | tf_op | source)
XLA Modules:
  0.0 35.4 jit_solution(16633482731168003249)
XLA Ops:
  0.0 1.8 %pack.1 = (f32[4,136,128]{2,1,0:T(8,128)}, f32[1024,128]{1,0:T(8,128)S(1)}) custom-call(f32[32,512]{1,0:T(8,128)} %residual_ref.1, s32[1,512]{1,0:T(1,128)} %bitcast.9, f32[1024,128]{1,0:T(8,128)} %bitcast.8), custom_call_target="tpu_custom_call" | custom-call | tf_op jit(solution)/shard_map/pack/pallas_call | solution.py:218
  1.8 4.2 %all-to-all-start = ((f32[4,136,128]{2,1,0:T(8,128)}), f32[4,136,128]{2,1,0:T(8,128)S(1)}, u32[]{:S(2)}, u32[]{:S(2)}) async-start(f32[4,136,128]{2,1,0:T(8,128)} %get-tuple-element.11), calls=%async_computation | async-start | bytes 557056 | tf_op jit(solution)/shard_map/all_to_all | solution.py:234
  6.1 0.6 %collective-permute-start = (s32[2,256]{1,0:T(2,128)}, s32[2,256]{1,0:T(2,128)S(1)}, u32[]{:S(2)}, u32[]{:S(2)}) collective-permute-start(s32[2,256]{1,0:T(2,128)} %bitcast.6), channel_id=1, source_target_pairs={{4,8},{12,16},{20,24},{8,4},{16,12},{24,20},{5,9},{13,17},{21,25},... | collective-permute-start | bytes 6152 | tf_op jit(solution)/shard_map/ppermute | solution.py:235
  6.7 5.6 %all-to-all-done.own_ref = f32[4,136,128]{2,1,0:T(8,128)S(1)} async-done(((f32[4,136,128]{2,1,0:T(8,128)}), f32[4,136,128]{2,1,0:T(8,128)S(1)}, u32[]{:S(2)}, u32[]{:S(2)}) %all-to-all-start) | async-done | bytes 278560 | tf_op jit(solution)/shard_map/all_to_all | solution.py:234
  12.3 1.5 %coarse.1 = f32[8,4,16,128]{3,2,1,0:T(8,128)} custom-call(f32[4,136,128]{2,1,0:T(8,128)S(1)} %all-to-all-done.own_ref, f32[1024,128]{1,0:T(8,128)S(1)} %get-tuple-element.12.coarse_ref), custom_call_target="tpu_custom_call" | custom-call | flops 8000000000 | tf_op jit(solution)/shard_map/coarse/pallas_call | solution.py:237
  13.8 5.5 %all-to-all-start.1 = ((f32[32,16,128]{2,1,0:T(8,128)}), f32[32,16,128]{2,1,0:T(8,128)S(1)}, u32[]{:S(2)}, u32[]{:S(2)}) async-start(f32[32,16,128]{2,1,0:T(8,128)} %bitcast.2), calls=%async_computation.1 | async-start | bytes 524288 | tf_op jit(solution)/shard_map/all_to_all | solution.py:247
  19.4 0.0 collective-permute-done.lists_ref
  19.4 0.3 outer.1
  19.7 0.0 copy-start
  19.7 0.0 copy-start.1
  19.8 0.8 %collective-permute-start.1 = (f32[32,256]{1,0:T(8,128)S(1)}, f32[32,256]{1,0:T(8,128)S(1)}, u32[]{:S(2)}, u32[]{:S(2)}) collective-permute-start(f32[32,256]{1,0:T(8,128)S(1)} %outer.1), channel_id=1, source_target_pairs={{4,8},{12,16},{20,24},{8,4},{16,12},{24,20},{5,9},{13,17},{21,25},... | collective-permute-start | bytes 98312 | tf_op jit(solution)/shard_map/ppermute | solution.py:257
  20.6 4.5 %collective-permute-start.2 = (f32[4,136,128]{2,1,0:T(8,128)S(1)}, f32[4,136,128]{2,1,0:T(8,128)S(1)}, u32[]{:S(2)}, u32[]{:S(2)}) collective-permute-start(f32[4,136,128]{2,1,0:T(8,128)S(1)} %all-to-all-done.own_ref), channel_id=1, source_target_pairs={{0,4},{8,12},{16,20},{24,28},{4,0},{12,8},{20,16},{28,24},{1,5},{9... | collective-permute-start | bytes 835592 | tf_op jit(solution)/shard_map/ppermute | solution.py:258
  25.1 3.4 %owned.1 = (f32[32,512]{1,0:T(8,128)S(1)}, bf16[2,256,512]{2,1,0:T(8,128)(2,1)S(1)}, bf16[2,256,512]{2,1,0:T(8,128)(2,1)S(1)}, bf16[256,512]{1,0:T(8,128)(2,1)S(1)}) custom-call(f32[4,136,128]{2,1,0:T(8,128)S(1)} %all-to-all-done.own_ref, s32[1,512]{1,0:T(1,128)} %bitcast.10, f32[1,2560,512]{2,1,0:T(8,128)} %fine_ref.1), custom_call_target="tpu_custom_call" | custom-call | flops 40000000000 | tf_op jit(solution)/shard_map/owned/pallas_call | solution.py:260
  28.5 4.2 %collective-permute-done.2.other_ref = f32[4,136,128]{2,1,0:T(8,128)S(1)} collective-permute-done((f32[4,136,128]{2,1,0:T(8,128)S(1)}, f32[4,136,128]{2,1,0:T(8,128)S(1)}, u32[]{:S(2)}, u32[]{:S(2)}) %collective-permute-start.2) | collective-permute-done | bytes 278560 | tf_op jit(solution)/shard_map/ppermute | solution.py:258
  32.7 0.0 copy-done
  32.7 0.0 copy-done.1
  32.7 1.1 %inner.1.total_ref = f32[32,512]{1,0:T(8,128)S(1)} custom-call(s32[1,2]{1,0:T(1,128)S(1)} %copy-done, f32[4,136,128]{2,1,0:T(8,128)S(1)} %collective-permute-done.2.other_ref, s32[2,256]{1,0:T(2,128)S(1)} %bitcast.7, bf16[2,256,512]{2,1,0:T(8,128)(2,1)S(1)} %get-tuple-element.13.hi_ref, bf16[2,256,512]{2,1,0:T(8,128)(2,1)S(1)} %get-tuple-element.14.low_ref, ...), custom_call_target="tpu_custom_call" | custom-call | tf_op jit(solution)/shard_map/inner/pallas_call | solution.py:280
  33.9 0.0 collective-permute-done.1.halo_ref
  33.9 0.0 all-to-all-done.1
  33.9 1.4 %tail.1 = f32[32,512]{1,0:T(8,128)} custom-call(s32[1,2]{1,0:T(1,128)S(1)} %copy-done, f32[8,4,16,128]{3,2,1,0:T(8,128)S(1)} %bitcast.5, f32[32,256]{1,0:T(8,128)S(1)} %collective-permute-done.1.halo_ref, bf16[2,256,512]{2,1,0:T(8,128)(2,1)S(1)} %get-tuple-element.13.hi_ref, bf16[2,256,512]{2,1,0:T(8,128)(2,1)S(1)} %get-tuple-element.14.low_ref, ...), custom_call_target="tpu_custom_call" | custom-call | tf_op jit(solution)/shard_map/tail/pallas_call | solution.py:289
Async XLA Ops:
  1.8 10.5 %all-to-all-start = ((f32[4,136,128]{2,1,0:T(8,128)}), f32[4,136,128]{2,1,0:T(8,128)S(1)}, u32[]{:S(2)}, u32[]{:S(2)}) async-start(f32[4,136,128]{2,1,0:T(8,128)} %get-tuple-element.11), calls=%async_computation | async-start | bytes 557056 | tf_op jit(solution)/shard_map/all_to_all | solution.py:234
  6.1 13.3 %collective-permute-start = (s32[2,256]{1,0:T(2,128)}, s32[2,256]{1,0:T(2,128)S(1)}, u32[]{:S(2)}, u32[]{:S(2)}) collective-permute-start(s32[2,256]{1,0:T(2,128)} %bitcast.6), channel_id=1, source_target_pairs={{4,8},{12,16},{20,24},{8,4},{16,12},{24,20},{5,9},{13,17},{21,25},... | collective-permute-start | bytes 6152 | tf_op jit(solution)/shard_map/ppermute | solution.py:235
  13.8 20.1 %all-to-all-start.1 = ((f32[32,16,128]{2,1,0:T(8,128)}), f32[32,16,128]{2,1,0:T(8,128)S(1)}, u32[]{:S(2)}, u32[]{:S(2)}) async-start(f32[32,16,128]{2,1,0:T(8,128)} %bitcast.2), calls=%async_computation.1 | async-start | bytes 524288 | tf_op jit(solution)/shard_map/all_to_all | solution.py:247
  19.7 13.0 %copy-start = (s32[1,2]{1,0:T(1,128)S(1)}, s32[1,2]{1,0:T(1,128)}, u32[]{:S(2)}) copy-start(s32[1,2]{1,0:T(1,128)} %counts_ref.3) | copy-start | bytes 28
  19.7 13.0 %copy-start.1 = (s32[1,2,256]{2,1,0:T(2,128)S(1)}, s32[1,2,256]{2,1,0:T(2,128)}, u32[]{:S(2)}) copy-start(s32[1,2,256]{2,1,0:T(2,128)} %param.9) | copy-start | bytes 6148
  19.8 14.1 %collective-permute-start.1 = (f32[32,256]{1,0:T(8,128)S(1)}, f32[32,256]{1,0:T(8,128)S(1)}, u32[]{:S(2)}, u32[]{:S(2)}) collective-permute-start(f32[32,256]{1,0:T(8,128)S(1)} %outer.1), channel_id=1, source_target_pairs={{4,8},{12,16},{20,24},{8,4},{16,12},{24,20},{5,9},{13,17},{21,25},... | collective-permute-start | bytes 98312 | tf_op jit(solution)/shard_map/ppermute | solution.py:257
  20.6 12.2 %collective-permute-start.2 = (f32[4,136,128]{2,1,0:T(8,128)S(1)}, f32[4,136,128]{2,1,0:T(8,128)S(1)}, u32[]{:S(2)}, u32[]{:S(2)}) collective-permute-start(f32[4,136,128]{2,1,0:T(8,128)S(1)} %all-to-all-done.own_ref), channel_id=1, source_target_pairs={{0,4},{8,12},{16,20},{24,28},{4,0},{12,8},{20,16},{28,24},{1,5},{9... | collective-permute-start | bytes 835592 | tf_op jit(solution)/shard_map/ppermute | solution.py:258

commit v3 on v2

v3 whole, which is shorter than its diff:
```python
import functools

import jax
import jax.numpy as jnp
from jax import lax
from jax.experimental import pallas as pl
from jax.experimental.pallas import tpu as pltpu
from jax.sharding import PartitionSpec as P

BF16 = jnp.bfloat16
F32 = jnp.float32
NN = (((1,), (0,)), ((), ()))
NT = (((1,), (1,)), ((), ()))
LANES = 128
MIB = 1 << 20


def split3(x):
    hi = x.astype(BF16)
    rest = x - hi.astype(F32)
    mid = rest.astype(BF16)
    low = (rest - mid.astype(F32)).astype(BF16)
    return jnp.concatenate([hi, mid, low], axis=0)


def split2(x):
    hi = x.astype(BF16)
    low = (x - hi.astype(F32)).astype(BF16)
    return hi, low


def dot(a, b, dims=NN):
    return lax.dot_general(a, b, dims, preferred_element_type=F32)


def dot_halves(x, w_hi, w_low):
    rows = x.shape[0]
    x_hi, x_low = split2(x)
    both = dot(jnp.concatenate([x_hi, x_low], axis=0), w_hi)
    return both[:rows] + both[rows:] + dot(x_hi, w_low)


def fold3(acc):
    rows = acc.shape[0] // 3
    return acc[:rows] + acc[rows : 2 * rows] + acc[2 * rows :]


def onehot(condition):
    return condition.astype(F32).astype(BF16)


def shard_rows(ref, shard, rows, tiles):
    return jnp.concatenate([ref[shard, pl.ds(t * rows, rows)] for t in range(tiles)], axis=1)


def pick(ref, rows, tiles, wanted):
    cols = tiles * LANES
    local = lax.broadcasted_iota(jnp.int32, (cols, wanted.shape[1]), 0)
    total = jnp.zeros((3 * rows, wanted.shape[1]), F32)
    for shard in range(ref.shape[0]):
        block = split3(shard_rows(ref, shard, rows, tiles))
        total = total + dot(block, onehot(local == wanted - shard * cols))
    return fold3(total)


def parity():
    return lax.rem(lax.axis_index("sub"), 2)


def pack_kernel(
    residual_ref, agg_ref, lists_ref, counts_ref, coarse_ref,
    out_ref, lists_out, coarse_out,
    residual_buf, agg_buf, lists_buf, counts_buf, packed_buf, sems,
):
    sources = (residual_ref, agg_ref, lists_ref, counts_ref, coarse_ref)
    targets = (residual_buf, agg_buf, lists_buf, counts_buf, coarse_out)
    fetches = [pltpu.make_async_copy(a, b, sems.at[k]) for k, (a, b) in enumerate(zip(sources, targets))]
    for fetch in fetches:
        fetch.start()
    rows, cols = residual_buf.shape
    tiles = cols // LANES
    fetches[0].wait()
    for t in range(tiles):
        packed_buf[t * rows : (t + 1) * rows] = residual_buf[:, t * LANES : (t + 1) * LANES]
    fetches[1].wait()
    codes = [agg_buf[:, t * LANES : (t + 1) * LANES].astype(F32) for t in range(tiles)]
    codes.append(jnp.zeros((packed_buf.shape[0] - rows * tiles - tiles, LANES), F32))
    packed_buf[rows * tiles :] = jnp.concatenate(codes, axis=0)
    sends = []
    for k in range(out_ref.shape[0]):
        sends.append(pltpu.make_async_copy(packed_buf, out_ref.at[k], sems.at[len(fetches) + k]))
        sends[k].start()
    fetches[2].wait()
    fetches[3].wait()
    slots = lax.broadcasted_iota(jnp.int32, (1, lists_buf.shape[1]), 1)
    for side in range(2):
        used = slots < counts_buf[:, side : side + 1]
        lists_out[side : side + 1] = jnp.where(used, lists_buf[side : side + 1], -1)
    fetches[4].wait()
    for send in sends:
        send.wait()


def coarse_kernel(width, rows, tiles, own_ref, coarse_ref, send_ref, chunk_buf, sems):
    shards = own_ref.shape[0]
    cols = tiles * LANES
    coarse_len = width * shards
    levels = lax.broadcasted_iota(jnp.int32, (coarse_len, cols), 0)
    rhs = jnp.zeros((3 * rows, coarse_len), F32)
    for shard in range(shards):
        block = split3(shard_rows(own_ref, shard, rows, tiles))
        codes = [own_ref[shard, pl.ds(tiles * rows + t, 1)] for t in range(tiles)]
        unknowns = jnp.concatenate(codes, axis=1).astype(jnp.int32)
        rhs = rhs + dot(block, onehot(levels == unknowns), NT)
    rhs = fold3(rhs)
    half = rows // 2
    lane = lax.broadcasted_iota(jnp.int32, (half, LANES), 1)
    stride = coarse_ref.shape[0] // coarse_len
    sends = []
    for tile in range(0, stride, 2):
        parts = [coarse_ref[pl.ds(tile + k, coarse_len, stride=stride), :] for k in range(2)]
        value = dot_halves(rhs, *split2(jnp.concatenate(parts, axis=1)))
        for k in range(2):
            part = value[:, k * LANES : (k + 1) * LANES]
            turned = pltpu.roll(part, width, 1)
            chunk_buf[2 * (tile + k)] = jnp.where(lane < width, part[:half], turned[half:])
            chunk_buf[2 * (tile + k) + 1] = jnp.where(lane < width, turned[:half], part[half:])
        ready = pl.ds(2 * tile, 4)
        for copy in range(shards):
            send = pltpu.make_async_copy(
                chunk_buf.at[ready], send_ref.at[ready, copy], sems.at[len(sends)]
            )
            send.start()
            sends.append(send)
    for send in sends:
        send.wait()


def margin_kernel(rows, tiles, own_ref, outer_lists_ref, inner_lists_ref, outer_ref, inner_ref):
    odd = parity()
    wanted = jnp.where(odd == 1, outer_lists_ref[0:1], outer_lists_ref[1:2])
    outer_ref[...] = pick(own_ref, rows, tiles, wanted)
    wanted = jnp.where(odd == 1, inner_lists_ref[1:2], inner_lists_ref[0:1])
    inner_ref[...] = pick(own_ref, rows, tiles, wanted)


def own_kernel(
    rows, tiles, margin, own_ref, agg_ref, fine_ref, out_ref, hi_ref, low_ref, hot_ref, agg_buf, fine_buf, sems
):
    shards = own_ref.shape[0]
    ext = fine_ref.shape[1]
    step = 2 * LANES
    starts = list(range(margin, ext - margin, step)) + [0, ext - margin]
    sizes = [step] * (len(starts) - 2) + [margin] * 2
    fetch = pltpu.make_async_copy(agg_ref, agg_buf, sems.at[len(starts)])
    fetch.start()
    copies = []
    for k, (start, size) in enumerate(zip(starts, sizes)):
        copies.append(
            pltpu.make_async_copy(
                fine_ref.at[0, pl.ds(start, size)], fine_buf.at[pl.ds(start, size)], sems.at[k]
            )
        )
        copies[k].start()
    fetch.wait()
    levels = lax.broadcasted_iota(jnp.int32, hot_ref.shape, 0)
    hot_ref[...] = onehot(levels == agg_buf[...])
    total = jnp.zeros(out_ref.shape, F32)
    for k, start in enumerate(starts[:-2]):
        shard, tile = divmod(2 * k, tiles)
        block = jnp.concatenate([own_ref[shard, pl.ds((tile + t) * rows, rows)] for t in range(2)], axis=1)
        copies[k].wait()
        total = total + dot_halves(block, *split2(fine_buf[start : start + step]))
    out_ref[...] = total
    for side in range(2):
        start = starts[side - 2]
        copies[side - 2].wait()
        hi_ref[side], low_ref[side] = split2(fine_buf[start : start + margin])


def tail_kernel(width, got_ref, outer_ref, inner_ref, hi_ref, low_ref, hot_ref, total_ref, out_ref):
    subs, shards, half, _ = got_ref.shape
    odd = parity()
    outer, inner = outer_ref[...], inner_ref[...]
    total = total_ref[...]
    total = total + dot_halves(jnp.where(odd == 1, inner, outer), hi_ref[0], low_ref[0])
    total = total + dot_halves(jnp.where(odd == 1, outer, inner), hi_ref[1], low_ref[1])
    sums = [got_ref[0, shard] for shard in range(shards)]
    for sub in range(1, subs):
        for shard in range(shards):
            sums[shard] = sums[shard] + got_ref[sub, shard]
    lane = lax.broadcasted_iota(jnp.int32, (half, LANES), 1)
    top, bottom = [], []
    for pair in range(shards // 2):
        left, right = sums[2 * pair], sums[2 * pair + 1]
        top.append(jnp.where(lane < width, left, pltpu.roll(right, width, 1)))
        bottom.append(jnp.where(lane < width, pltpu.roll(left, width, 1), right))
    coarse = jnp.concatenate([jnp.concatenate(top, axis=1), jnp.concatenate(bottom, axis=1)], axis=0)
    out_ref[...] = total + fold3(dot(split3(coarse), hot_ref[...]))


def whole(space=pltpu.VMEM):
    return pl.BlockSpec(memory_space=space)


def limit(mib):
    return pltpu.CompilerParams(vmem_limit_bytes=mib * MIB)


def in_hbm(x):
    return pltpu.with_memory_space_constraint(x, pltpu.HBM)


def weight(flops):
    return pl.CostEstimate(flops=flops, bytes_accessed=0, transcendentals=0)


def on_device(residual, fine_inverse, coarse_inverse, wanted_rows, wanted_count, aggregate):
    subs = lax.axis_size("sub")
    shards = lax.axis_size("blk")
    rows, cols = residual.shape
    tiles = cols // LANES
    margin = wanted_rows.shape[2]
    coarse_len = coarse_inverse.shape[0]
    width = coarse_len // shards
    packed_rows = -(-(rows * tiles + tiles) // 8) * 8
    inner = [(i, i + 1) for i in range(0, subs, 2)] + [(i + 1, i) for i in range(0, subs, 2)]
    outer = [(i, i + 1) for i in range(1, subs - 1, 2)] + [(i + 1, i) for i in range(1, subs - 1, 2)]
    codes = aggregate[None]
    lists = wanted_rows[0]
    table = coarse_inverse.reshape(-1, LANES)
    packed_shape = (packed_rows, LANES)

    packed, lists, table = pl.pallas_call(
        pack_kernel,
        out_shape=(
            jax.ShapeDtypeStruct((shards,) + packed_shape, F32),
            jax.ShapeDtypeStruct(lists.shape, jnp.int32),
            jax.ShapeDtypeStruct(table.shape, F32),
        ),
        in_specs=[whole(pl.ANY)] * 5,
        out_specs=(whole(pl.ANY), whole(), whole()),
        scratch_shapes=[
            pltpu.VMEM(residual.shape, F32),
            pltpu.VMEM(codes.shape, jnp.int32),
            pltpu.VMEM(lists.shape, jnp.int32),
            pltpu.VMEM(wanted_count.shape, jnp.int32),
            pltpu.VMEM(packed_shape, F32),
            pltpu.SemaphoreType.DMA((5 + shards,)),
        ],
        compiler_params=limit(4),
        name="pack",
    )(in_hbm(residual), in_hbm(codes), in_hbm(lists), in_hbm(wanted_count), in_hbm(table))
    own = lax.all_to_all(packed, "blk", 0, 0, tiled=True)
    outer_lists = lax.ppermute(lists, "sub", outer)
    inner_lists = lax.ppermute(lists, "sub", inner)

    send = pl.pallas_call(
        functools.partial(coarse_kernel, width, rows, tiles),
        out_shape=jax.ShapeDtypeStruct((subs, shards, rows // 2, LANES), F32),
        in_specs=[whole()] * 2,
        out_specs=whole(pl.ANY),
        scratch_shapes=[
            pltpu.VMEM((subs, rows // 2, LANES), F32),
            pltpu.SemaphoreType.DMA((shards * subs // 4,)),
        ],
        compiler_params=limit(12),
        cost_estimate=weight(8 * 10**9),
        name="coarse",
    )(own, table)
    flat = send.reshape((subs * shards,) + send.shape[2:])
    got = lax.all_to_all(flat, ("sub", "blk"), 0, 0, tiled=True).reshape(send.shape)

    outgoing, ingoing = pl.pallas_call(
        functools.partial(margin_kernel, rows, tiles),
        out_shape=(jax.ShapeDtypeStruct((rows, margin), F32),) * 2,
        in_specs=[whole()] * 3,
        out_specs=(whole(), whole()),
        compiler_params=limit(8),
        cost_estimate=weight(4 * 10**9),
        name="margins",
    )(own, outer_lists, inner_lists)
    outer_halo = lax.ppermute(outgoing, "sub", outer)
    inner_halo = lax.ppermute(ingoing, "sub", inner)

    owned, w_hi, w_low, hot = pl.pallas_call(
        functools.partial(own_kernel, rows, tiles, margin),
        out_shape=(
            jax.ShapeDtypeStruct((rows, cols), F32),
            jax.ShapeDtypeStruct((2, margin, cols), BF16),
            jax.ShapeDtypeStruct((2, margin, cols), BF16),
            jax.ShapeDtypeStruct((coarse_len, cols), BF16),
        ),
        in_specs=[whole(), whole(pl.ANY), whole(pl.ANY)],
        out_specs=(whole(),) * 4,
        scratch_shapes=[
            pltpu.VMEM(codes.shape, jnp.int32),
            pltpu.VMEM(fine_inverse.shape[1:], F32),
            pltpu.SemaphoreType.DMA((shards * tiles // 2 + 3,)),
        ],
        compiler_params=limit(16),
        cost_estimate=weight(40 * 10**9),
        name="owned",
    )(own, in_hbm(codes), in_hbm(fine_inverse))

    return pl.pallas_call(
        functools.partial(tail_kernel, width),
        out_shape=jax.ShapeDtypeStruct((rows, cols), F32),
        in_specs=[whole()] * 7,
        out_specs=whole(),
        compiler_params=limit(12),
        name="tail",
    )(got, outer_halo, inner_halo, w_hi, w_low, hot, owned)


def solution(mesh):
    in_specs = (
        P(None, ("sub", "blk")),
        P("sub", None, "blk"),
        P("sub", "blk", None),
        P("sub", None, None),
        P("sub", None),
        P(("sub", "blk")),
    )
    out_specs = P(None, ("sub", "blk"))
    return jax.shard_map(
        on_device, mesh=mesh, in_specs=in_specs, out_specs=out_specs, check_vma=False
    )
```

time: 35.7 us -> 31.1 us (0.87)
  waiting for transfers between devices: 9.76 us -> 5.53 us
  Pallas kernels: 9.71 us -> 7.32 us
  starting transfers between devices: 15.8 us -> 17.9 us
    ppermute x3 -> x4, waiting for transfers between devices: 4.21 us -> 0.01 us  [the longest x1 0.01 us: on_device(): inner_lists = lax.ppermute(lists, 'sub', inner)]
    all_to_all x1, waiting for transfers between devices: 5.56 us -> 3.33 us  [on_device(): own = lax.all_to_all(packed, 'blk', 0, 0, tiled=True)]
    all_to_all x1, waiting for transfers between devices: 0.01 us -> 2.19 us  [on_device(): lax.all_to_all(flat, ('sub', 'blk'), 0, 0, tiled=True).reshape(send.shape)]
    ppermute x3 -> x4, starting transfers between devices: 5.99 us -> 8.09 us  [the longest x1 4.54 us: on_device(): inner_halo = lax.ppermute(ingoing, 'sub', inner)]
    pallas_call x3 -> x2, Pallas kernels: 3.3 us -> 2.11 us  [the longest x1 1.64 us: on_device(): pl.pallas_call(pack_kernel, out_shape=(jax.ShapeDtypeStruct((shards,) + p...]
    pallas_call x1, Pallas kernels: 3.43 us -> 2.66 us  [on_device(): pl.pallas_call(functools.partial(own_kernel, rows, tiles, margin), out_sh...]
    pallas_call x1, Pallas kernels: 1.45 us -> 0.98 us  [on_device(): pl.pallas_call(functools.partial(tail_kernel, width), out_shape=jax.Shape...]
  transfers between devices with their start and end apart: 5 -> 6, of which waited for: 2 -> 2; matrix products, arithmetic and copies ran while one was open for 0% -> 0% of each run, Pallas kernels for 18% -> 15%
where the time goes in v3:
time: 31.1 us; the launch traced here: 30.8 us
  starting transfers between devices  17.9 us (58%)
  Pallas kernels  7.32 us (24%)
  waiting for transfers between devices  5.53 us (18%)
    all_to_all x1, starting transfers between devices, on_device(): lax.all_to_all(flat, ('sub', 'blk'), 0, 0, tiled=True).reshape(send.shape)  5.53 us
    ppermute x1, starting transfers between devices, on_device(): inner_halo = lax.ppermute(ingoing, 'sub', inner)  4.54 us
    all_to_all x1, starting transfers between devices, on_device(): own = lax.all_to_all(packed, 'blk', 0, 0, tiled=True)  4.25 us
    all_to_all x1, waiting for transfers between devices, on_device(): own = lax.all_to_all(packed, 'blk', 0, 0, tiled=True)  3.33 us
    pallas_call x1, Pallas kernels, on_device(): pl.pallas_call(functools.partial(own_kernel, rows, tiles, margin), out_sh...  2.66 us
    ppermute x1, starting transfers between devices, on_device(): inner_lists = lax.ppermute(lists, 'sub', inner)  2.22 us
    all_to_all x1, waiting for transfers between devices, on_device(): lax.all_to_all(flat, ('sub', 'blk'), 0, 0, tiled=True).reshape(send.shape)  2.19 us
    pallas_call x1, Pallas kernels, on_device(): pl.pallas_call(pack_kernel, out_shape=(jax.ShapeDtypeStruct((shards,) + p...  1.64 us
  transfers between devices with their start and end apart: 6, of which 2 were waited for; matrix products, arithmetic and copies ran while one was open for 0% of the time, Pallas kernels for 15%

profile of v3, /device:TPU:0, one launch (start us, length us, event | category | flops | bytes accessed | tf_op | source)
XLA Modules:
  0.0 30.8 jit_solution(1636683375173418585)
XLA Ops:
  0.0 1.6 %pack.1 = (f32[4,136,128]{2,1,0:T(8,128)}, s32[2,256]{1,0:T(2,128)S(1)}, f32[1024,128]{1,0:T(8,128)S(1)}) custom-call(f32[32,512]{1,0:T(8,128)} %residual_ref.1, s32[1,512]{1,0:T(1,128)} %bitcast.8, s32[2,256]{1,0:T(2,128)} %bitcast.7, s32[1,2]{1,0:T(1,128)} %counts_ref.1, f32[1024,128]{1,0:T(8,128)} %bitcast.6), custom_call_target="tpu_custom_call" | custom-call | tf_op jit(solution)/shard_map/pack/pallas_call | solution.py:234
  1.6 4.2 %all-to-all-start = ((f32[4,136,128]{2,1,0:T(8,128)}), f32[4,136,128]{2,1,0:T(8,128)S(1)}, u32[]{:S(2)}, u32[]{:S(2)}) async-start(f32[4,136,128]{2,1,0:T(8,128)} %get-tuple-element.14), calls=%async_computation | async-start | bytes 557056 | tf_op jit(solution)/shard_map/all_to_all | solution.py:254
  5.9 2.2 %collective-permute-start.1 = (s32[2,256]{1,0:T(2,128)S(1)}, s32[2,256]{1,0:T(2,128)S(1)}, u32[]{:S(2)}, u32[]{:S(2)}) collective-permute-start(s32[2,256]{1,0:T(2,128)S(1)} %get-tuple-element.16), channel_id=1, source_target_pairs={{0,4},{8,12},{16,20},{24,28},{4,0},{12,8},{20,16},{28,24},{1,5},{9... | collective-permute-start | bytes 6152 | tf_op jit(solution)/shard_map/ppermute | solution.py:256
  8.1 0.6 %collective-permute-start = (s32[2,256]{1,0:T(2,128)S(1)}, s32[2,256]{1,0:T(2,128)S(1)}, u32[]{:S(2)}, u32[]{:S(2)}) collective-permute-start(s32[2,256]{1,0:T(2,128)S(1)} %get-tuple-element.16), channel_id=1, source_target_pairs={{4,8},{12,16},{20,24},{8,4},{16,12},{24,20},{5,9},{13,17},{21,25},... | collective-permute-start | bytes 6152 | tf_op jit(solution)/shard_map/ppermute | solution.py:255
  8.8 3.3 %all-to-all-done.own_ref = f32[4,136,128]{2,1,0:T(8,128)S(1)} async-done(((f32[4,136,128]{2,1,0:T(8,128)}), f32[4,136,128]{2,1,0:T(8,128)S(1)}, u32[]{:S(2)}, u32[]{:S(2)}) %all-to-all-start) | async-done | bytes 278560 | tf_op jit(solution)/shard_map/all_to_all | solution.py:254
  12.1 1.6 %coarse.1 = f32[8,4,16,128]{3,2,1,0:T(8,128)} custom-call(f32[4,136,128]{2,1,0:T(8,128)S(1)} %all-to-all-done.own_ref, f32[1024,128]{1,0:T(8,128)S(1)} %get-tuple-element.15.coarse_ref), custom_call_target="tpu_custom_call" | custom-call | flops 8000000000 | tf_op jit(solution)/shard_map/coarse/pallas_call | solution.py:258
  13.7 5.5 %all-to-all-start.1 = ((f32[32,16,128]{2,1,0:T(8,128)}), f32[32,16,128]{2,1,0:T(8,128)S(1)}, u32[]{:S(2)}, u32[]{:S(2)}) async-start(f32[32,16,128]{2,1,0:T(8,128)} %bitcast.3), calls=%async_computation.1 | async-start | bytes 524288 | tf_op jit(solution)/shard_map/all_to_all | solution.py:272
  19.2 0.0 collective-permute-done.1.inner_lists_ref
  19.2 0.0 collective-permute-done.outer_lists_ref
  19.2 0.5 %margins.1 = (f32[32,256]{1,0:T(8,128)S(1)}, f32[32,256]{1,0:T(8,128)S(1)}) custom-call(f32[4,136,128]{2,1,0:T(8,128)S(1)} %all-to-all-done.own_ref, s32[2,256]{1,0:T(2,128)S(1)} %collective-permute-done.outer_lists_ref, s32[2,256]{1,0:T(2,128)S(1)} %collective-permute-done.1.inner_lists_ref), custom_call_target="tpu_custom_call" | custom-call | flops 4000000000 | tf_op jit(solution)/shard_map/margins/pallas_call | solution.py:274
  19.7 0.7 %collective-permute-start.2 = (f32[32,256]{1,0:T(8,128)S(1)}, f32[32,256]{1,0:T(8,128)S(1)}, u32[]{:S(2)}, u32[]{:S(2)}) collective-permute-start(f32[32,256]{1,0:T(8,128)S(1)} %get-tuple-element.17), channel_id=1, source_target_pairs={{4,8},{12,16},{20,24},{8,4},{16,12},{24,20},{5,9},{13,17},{21,25},... | collective-permute-start | bytes 98312 | tf_op jit(solution)/shard_map/ppermute | solution.py:283
  20.4 4.5 %collective-permute-start.3 = (f32[32,256]{1,0:T(8,128)S(1)}, f32[32,256]{1,0:T(8,128)S(1)}, u32[]{:S(2)}, u32[]{:S(2)}) collective-permute-start(f32[32,256]{1,0:T(8,128)S(1)} %get-tuple-element.18), channel_id=1, source_target_pairs={{0,4},{8,12},{16,20},{24,28},{4,0},{12,8},{20,16},{28,24},{1,5},{9... | collective-permute-start | bytes 98312 | tf_op jit(solution)/shard_map/ppermute | solution.py:284
  24.9 2.7 %owned.1 = (f32[32,512]{1,0:T(8,128)S(1)}, bf16[2,256,512]{2,1,0:T(8,128)(2,1)S(1)}, bf16[2,256,512]{2,1,0:T(8,128)(2,1)S(1)}, bf16[256,512]{1,0:T(8,128)(2,1)S(1)}) custom-call(f32[4,136,128]{2,1,0:T(8,128)S(1)} %all-to-all-done.own_ref, s32[1,512]{1,0:T(1,128)} %bitcast.9, f32[1,2560,512]{2,1,0:T(8,128)} %fine_ref.1), custom_call_target="tpu_custom_call" | custom-call | flops 40000000000 | tf_op jit(solution)/shard_map/owned/pallas_call | solution.py:286
  27.6 0.0 collective-permute-done.2.outer_ref
  27.6 0.0 collective-permute-done.3.inner_ref
  27.6 2.2 %all-to-all-done.1 = f32[32,16,128]{2,1,0:T(8,128)S(1)} async-done(((f32[32,16,128]{2,1,0:T(8,128)}), f32[32,16,128]{2,1,0:T(8,128)S(1)}, u32[]{:S(2)}, u32[]{:S(2)}) %all-to-all-start.1) | async-done | bytes 262176 | tf_op jit(solution)/shard_map/all_to_all | solution.py:272
  29.8 1.0 %tail.1 = f32[32,512]{1,0:T(8,128)} custom-call(f32[8,4,16,128]{3,2,1,0:T(8,128)S(1)} %bitcast.5, f32[32,256]{1,0:T(8,128)S(1)} %collective-permute-done.2.outer_ref, f32[32,256]{1,0:T(8,128)S(1)} %collective-permute-done.3.inner_ref, bf16[2,256,512]{2,1,0:T(8,128)(2,1)S(1)} %get-tuple-element.19.hi_ref, bf16[2,256,512]{2,1,0:T(8,128)(2,1)S(1)} %get-tuple-element.20.low_ref, ...), custom_call_target="tpu_custom_call" | custom-call | tf_op jit(solution)/shard_map/tail/pallas_call | solution.py:306
Async XLA Ops:
  1.6 10.5 %all-to-all-start = ((f32[4,136,128]{2,1,0:T(8,128)}), f32[4,136,128]{2,1,0:T(8,128)S(1)}, u32[]{:S(2)}, u32[]{:S(2)}) async-start(f32[4,136,128]{2,1,0:T(8,128)} %get-tuple-element.14), calls=%async_computation | async-start | bytes 557056 | tf_op jit(solution)/shard_map/all_to_all | solution.py:254
  5.9 13.3 %collective-permute-start.1 = (s32[2,256]{1,0:T(2,128)S(1)}, s32[2,256]{1,0:T(2,128)S(1)}, u32[]{:S(2)}, u32[]{:S(2)}) collective-permute-start(s32[2,256]{1,0:T(2,128)S(1)} %get-tuple-element.16), channel_id=1, source_target_pairs={{0,4},{8,12},{16,20},{24,28},{4,0},{12,8},{20,16},{28,24},{1,5},{9... | collective-permute-start | bytes 6152 | tf_op jit(solution)/shard_map/ppermute | solution.py:256
  8.1 11.1 %collective-permute-start = (s32[2,256]{1,0:T(2,128)S(1)}, s32[2,256]{1,0:T(2,128)S(1)}, u32[]{:S(2)}, u32[]{:S(2)}) collective-permute-start(s32[2,256]{1,0:T(2,128)S(1)} %get-tuple-element.16), channel_id=1, source_target_pairs={{4,8},{12,16},{20,24},{8,4},{16,12},{24,20},{5,9},{13,17},{21,25},... | collective-permute-start | bytes 6152 | tf_op jit(solution)/shard_map/ppermute | solution.py:255
  13.7 16.1 %all-to-all-start.1 = ((f32[32,16,128]{2,1,0:T(8,128)}), f32[32,16,128]{2,1,0:T(8,128)S(1)}, u32[]{:S(2)}, u32[]{:S(2)}) async-start(f32[32,16,128]{2,1,0:T(8,128)} %bitcast.3), calls=%async_computation.1 | async-start | bytes 524288 | tf_op jit(solution)/shard_map/all_to_all | solution.py:272
  19.7 7.9 %collective-permute-start.2 = (f32[32,256]{1,0:T(8,128)S(1)}, f32[32,256]{1,0:T(8,128)S(1)}, u32[]{:S(2)}, u32[]{:S(2)}) collective-permute-start(f32[32,256]{1,0:T(8,128)S(1)} %get-tuple-element.17), channel_id=1, source_target_pairs={{4,8},{12,16},{20,24},{8,4},{16,12},{24,20},{5,9},{13,17},{21,25},... | collective-permute-start | bytes 98312 | tf_op jit(solution)/shard_map/ppermute | solution.py:283
  20.4 7.2 %collective-permute-start.3 = (f32[32,256]{1,0:T(8,128)S(1)}, f32[32,256]{1,0:T(8,128)S(1)}, u32[]{:S(2)}, u32[]{:S(2)}) collective-permute-start(f32[32,256]{1,0:T(8,128)S(1)} %get-tuple-element.18), channel_id=1, source_target_pairs={{0,4},{8,12},{16,20},{24,28},{4,0},{12,8},{20,16},{28,24},{1,5},{9... | collective-permute-start | bytes 98312 | tf_op jit(solution)/shard_map/ppermute | solution.py:284

commit v4 on v3

--- a/solution.py
+++ b/solution.py
@@ -101,7 +101,7 @@
         send.wait()
 
 
-def coarse_kernel(width, rows, tiles, own_ref, coarse_ref, send_ref, chunk_buf, sems):
+def coarse_kernel(width, rows, tiles, slots, own_ref, coarse_ref, send_ref, chunk_buf, sems):
     shards = own_ref.shape[0]
     cols = tiles * LANES
     coarse_len = width * shards
@@ -125,13 +125,13 @@
             turned = pltpu.roll(part, width, 1)
             chunk_buf[2 * (tile + k)] = jnp.where(lane < width, part[:half], turned[half:])
             chunk_buf[2 * (tile + k) + 1] = jnp.where(lane < width, turned[:half], part[half:])
-        ready = pl.ds(2 * tile, 4)
-        for copy in range(shards):
-            send = pltpu.make_async_copy(
-                chunk_buf.at[ready], send_ref.at[ready, copy], sems.at[len(sends)]
-            )
-            send.start()
-            sends.append(send)
+        for sub in range(2 * tile, 2 * tile + 4):
+            for copy in range(shards):
+                send = pltpu.make_async_copy(
+                    chunk_buf.at[sub], send_ref.at[slots[sub], copy], sems.at[len(sends)]
+                )
+                send.start()
+                sends.append(send)
     for send in sends:
         send.wait()
 
@@ -226,6 +226,8 @@
     packed_rows = -(-(rows * tiles + tiles) // 8) * 8
     inner = [(i, i + 1) for i in range(0, subs, 2)] + [(i + 1, i) for i in range(0, subs, 2)]
     outer = [(i, i + 1) for i in range(1, subs - 1, 2)] + [(i + 1, i) for i in range(1, subs - 1, 2)]
+    receivers = [sub for k in range(subs // 2) for sub in (k, subs - 1 - k)]
+    slots = [receivers.index(sub) for sub in range(subs)]
     codes = aggregate[None]
     lists = wanted_rows[0]
     table = coarse_inverse.reshape(-1, LANES)
@@ -256,20 +258,22 @@
     inner_lists = lax.ppermute(lists, "sub", inner)
 
     send = pl.pallas_call(
-        functools.partial(coarse_kernel, width, rows, tiles),
+        functools.partial(coarse_kernel, width, rows, tiles, slots),
         out_shape=jax.ShapeDtypeStruct((subs, shards, rows // 2, LANES), F32),
         in_specs=[whole()] * 2,
         out_specs=whole(pl.ANY),
         scratch_shapes=[
             pltpu.VMEM((subs, rows // 2, LANES), F32),
-            pltpu.SemaphoreType.DMA((shards * subs // 4,)),
+            pltpu.SemaphoreType.DMA((shards * subs,)),
         ],
         compiler_params=limit(12),
         cost_estimate=weight(8 * 10**9),
         name="coarse",
     )(own, table)
     flat = send.reshape((subs * shards,) + send.shape[2:])
-    got = lax.all_to_all(flat, ("sub", "blk"), 0, 0, tiled=True).reshape(send.shape)
+    members = [sub * shards + shard for sub in receivers for shard in range(shards)]
+    got = lax.all_to_all(flat, ("sub", "blk"), 0, 0, axis_index_groups=[members], tiled=True)
+    got = got.reshape(send.shape)
 
     outgoing, ingoing = pl.pallas_call(
         functools.partial(margin_kernel, rows, tiles),

time: 31.1 us -> 31.2 us (level)
  transfers between devices with their start and end apart: 6 -> 6, of which waited for: 2 -> 2; matrix products, arithmetic and copies ran while one was open for 0% -> 0% of each run, Pallas kernels for 15% -> 16%
where the time goes in v4:
time: 31.2 us; the launch traced here: 31 us
  starting transfers between devices  17.9 us (57%)
  Pallas kernels  7.53 us (24%)
  waiting for transfers between devices  5.47 us (18%)
    all_to_all x1, starting transfers between devices, on_device(): lax.all_to_all(flat, ('sub', 'blk'), 0, 0, axis_index_groups=[members], t...  5.53 us
    ppermute x1, starting transfers between devices, on_device(): inner_halo = lax.ppermute(ingoing, 'sub', inner)  4.54 us
    all_to_all x1, starting transfers between devices, on_device(): own = lax.all_to_all(packed, 'blk', 0, 0, tiled=True)  4.25 us
    all_to_all x1, waiting for transfers between devices, on_device(): own = lax.all_to_all(packed, 'blk', 0, 0, tiled=True)  3.33 us
    pallas_call x1, Pallas kernels, on_device(): pl.pallas_call(functools.partial(own_kernel, rows, tiles, margin), out_sh...  2.66 us
    ppermute x1, starting transfers between devices, on_device(): inner_lists = lax.ppermute(lists, 'sub', inner)  2.22 us
    all_to_all x1, waiting for transfers between devices, on_device(): lax.all_to_all(flat, ('sub', 'blk'), 0, 0, axis_index_groups=[members], t...  2.13 us
    pallas_call x1, Pallas kernels, on_device(): pl.pallas_call(functools.partial(coarse_kernel, width, rows, tiles, slots...  1.78 us
  transfers between devices with their start and end apart: 6, of which 2 were waited for; matrix products, arithmetic and copies ran while one was open for 0% of the time, Pallas kernels for 16%

profile of v4, /device:TPU:0, one launch (start us, length us, event | category | flops | bytes accessed | tf_op | source)
XLA Modules:
  0.0 31.0 jit_solution(8403706439841782040)
XLA Ops:
  0.0 1.6 %pack.1 = (f32[4,136,128]{2,1,0:T(8,128)}, s32[2,256]{1,0:T(2,128)S(1)}, f32[1024,128]{1,0:T(8,128)S(1)}) custom-call(f32[32,512]{1,0:T(8,128)} %residual_ref.1, s32[1,512]{1,0:T(1,128)} %bitcast.8, s32[2,256]{1,0:T(2,128)} %bitcast.7, s32[1,2]{1,0:T(1,128)} %counts_ref.1, f32[1024,128]{1,0:T(8,128)} %bitcast.6), custom_call_target="tpu_custom_call" | custom-call | tf_op jit(solution)/shard_map/pack/pallas_call | solution.py:236
  1.6 4.2 %all-to-all-start = ((f32[4,136,128]{2,1,0:T(8,128)}), f32[4,136,128]{2,1,0:T(8,128)S(1)}, u32[]{:S(2)}, u32[]{:S(2)}) async-start(f32[4,136,128]{2,1,0:T(8,128)} %get-tuple-element.14), calls=%async_computation | async-start | bytes 557056 | tf_op jit(solution)/shard_map/all_to_all | solution.py:256
  5.9 2.2 %collective-permute-start.1 = (s32[2,256]{1,0:T(2,128)S(1)}, s32[2,256]{1,0:T(2,128)S(1)}, u32[]{:S(2)}, u32[]{:S(2)}) collective-permute-start(s32[2,256]{1,0:T(2,128)S(1)} %get-tuple-element.16), channel_id=1, source_target_pairs={{0,4},{8,12},{16,20},{24,28},{4,0},{12,8},{20,16},{28,24},{1,5},{9... | collective-permute-start | bytes 6152 | tf_op jit(solution)/shard_map/ppermute | solution.py:258
  8.1 0.6 %collective-permute-start = (s32[2,256]{1,0:T(2,128)S(1)}, s32[2,256]{1,0:T(2,128)S(1)}, u32[]{:S(2)}, u32[]{:S(2)}) collective-permute-start(s32[2,256]{1,0:T(2,128)S(1)} %get-tuple-element.16), channel_id=1, source_target_pairs={{4,8},{12,16},{20,24},{8,4},{16,12},{24,20},{5,9},{13,17},{21,25},... | collective-permute-start | bytes 6152 | tf_op jit(solution)/shard_map/ppermute | solution.py:257
  8.8 3.3 %all-to-all-done.own_ref = f32[4,136,128]{2,1,0:T(8,128)S(1)} async-done(((f32[4,136,128]{2,1,0:T(8,128)}), f32[4,136,128]{2,1,0:T(8,128)S(1)}, u32[]{:S(2)}, u32[]{:S(2)}) %all-to-all-start) | async-done | bytes 278560 | tf_op jit(solution)/shard_map/all_to_all | solution.py:256
  12.1 1.8 %coarse.1 = f32[8,4,16,128]{3,2,1,0:T(8,128)} custom-call(f32[4,136,128]{2,1,0:T(8,128)S(1)} %all-to-all-done.own_ref, f32[1024,128]{1,0:T(8,128)S(1)} %get-tuple-element.15.coarse_ref), custom_call_target="tpu_custom_call" | custom-call | flops 8000000000 | tf_op jit(solution)/shard_map/coarse/pallas_call | solution.py:260
  13.9 5.5 %all-to-all-start.1 = ((f32[32,16,128]{2,1,0:T(8,128)}), f32[32,16,128]{2,1,0:T(8,128)S(1)}, u32[]{:S(2)}, u32[]{:S(2)}) async-start(f32[32,16,128]{2,1,0:T(8,128)} %bitcast.3), calls=%async_computation.1 | async-start | bytes 524288 | tf_op jit(solution)/shard_map/all_to_all | solution.py:275
  19.4 0.0 collective-permute-done.1.inner_lists_ref
  19.4 0.0 collective-permute-done.outer_lists_ref
  19.5 0.5 %margins.1 = (f32[32,256]{1,0:T(8,128)S(1)}, f32[32,256]{1,0:T(8,128)S(1)}) custom-call(f32[4,136,128]{2,1,0:T(8,128)S(1)} %all-to-all-done.own_ref, s32[2,256]{1,0:T(2,128)S(1)} %collective-permute-done.outer_lists_ref, s32[2,256]{1,0:T(2,128)S(1)} %collective-permute-done.1.inner_lists_ref), custom_call_target="tpu_custom_call" | custom-call | flops 4000000000 | tf_op jit(solution)/shard_map/margins/pallas_call | solution.py:278
  19.9 0.7 %collective-permute-start.2 = (f32[32,256]{1,0:T(8,128)S(1)}, f32[32,256]{1,0:T(8,128)S(1)}, u32[]{:S(2)}, u32[]{:S(2)}) collective-permute-start(f32[32,256]{1,0:T(8,128)S(1)} %get-tuple-element.17), channel_id=1, source_target_pairs={{4,8},{12,16},{20,24},{8,4},{16,12},{24,20},{5,9},{13,17},{21,25},... | collective-permute-start | bytes 98312 | tf_op jit(solution)/shard_map/ppermute | solution.py:287
  20.6 4.5 %collective-permute-start.3 = (f32[32,256]{1,0:T(8,128)S(1)}, f32[32,256]{1,0:T(8,128)S(1)}, u32[]{:S(2)}, u32[]{:S(2)}) collective-permute-start(f32[32,256]{1,0:T(8,128)S(1)} %get-tuple-element.18), channel_id=1, source_target_pairs={{0,4},{8,12},{16,20},{24,28},{4,0},{12,8},{20,16},{28,24},{1,5},{9... | collective-permute-start | bytes 98312 | tf_op jit(solution)/shard_map/ppermute | solution.py:288
  25.2 2.7 %owned.1 = (f32[32,512]{1,0:T(8,128)S(1)}, bf16[2,256,512]{2,1,0:T(8,128)(2,1)S(1)}, bf16[2,256,512]{2,1,0:T(8,128)(2,1)S(1)}, bf16[256,512]{1,0:T(8,128)(2,1)S(1)}) custom-call(f32[4,136,128]{2,1,0:T(8,128)S(1)} %all-to-all-done.own_ref, s32[1,512]{1,0:T(1,128)} %bitcast.9, f32[1,2560,512]{2,1,0:T(8,128)} %fine_ref.1), custom_call_target="tpu_custom_call" | custom-call | flops 40000000000 | tf_op jit(solution)/shard_map/owned/pallas_call | solution.py:290
  27.8 0.0 collective-permute-done.2.outer_ref
  27.8 0.0 collective-permute-done.3.inner_ref
  27.8 2.1 %all-to-all-done.1 = f32[32,16,128]{2,1,0:T(8,128)S(1)} async-done(((f32[32,16,128]{2,1,0:T(8,128)}), f32[32,16,128]{2,1,0:T(8,128)S(1)}, u32[]{:S(2)}, u32[]{:S(2)}) %all-to-all-start.1) | async-done | bytes 262176 | tf_op jit(solution)/shard_map/all_to_all | solution.py:275
  30.0 1.0 %tail.1 = f32[32,512]{1,0:T(8,128)} custom-call(f32[8,4,16,128]{3,2,1,0:T(8,128)S(1)} %bitcast.5, f32[32,256]{1,0:T(8,128)S(1)} %collective-permute-done.2.outer_ref, f32[32,256]{1,0:T(8,128)S(1)} %collective-permute-done.3.inner_ref, bf16[2,256,512]{2,1,0:T(8,128)(2,1)S(1)} %get-tuple-element.19.hi_ref, bf16[2,256,512]{2,1,0:T(8,128)(2,1)S(1)} %get-tuple-element.20.low_ref, ...), custom_call_target="tpu_custom_call" | custom-call | tf_op jit(solution)/shard_map/tail/pallas_call | solution.py:310
Async XLA Ops:
  1.6 10.5 %all-to-all-start = ((f32[4,136,128]{2,1,0:T(8,128)}), f32[4,136,128]{2,1,0:T(8,128)S(1)}, u32[]{:S(2)}, u32[]{:S(2)}) async-start(f32[4,136,128]{2,1,0:T(8,128)} %get-tuple-element.14), calls=%async_computation | async-start | bytes 557056 | tf_op jit(solution)/shard_map/all_to_all | solution.py:256
  5.9 13.5 %collective-permute-start.1 = (s32[2,256]{1,0:T(2,128)S(1)}, s32[2,256]{1,0:T(2,128)S(1)}, u32[]{:S(2)}, u32[]{:S(2)}) collective-permute-start(s32[2,256]{1,0:T(2,128)S(1)} %get-tuple-element.16), channel_id=1, source_target_pairs={{0,4},{8,12},{16,20},{24,28},{4,0},{12,8},{20,16},{28,24},{1,5},{9... | collective-permute-start | bytes 6152 | tf_op jit(solution)/shard_map/ppermute | solution.py:258
  8.1 11.3 %collective-permute-start = (s32[2,256]{1,0:T(2,128)S(1)}, s32[2,256]{1,0:T(2,128)S(1)}, u32[]{:S(2)}, u32[]{:S(2)}) collective-permute-start(s32[2,256]{1,0:T(2,128)S(1)} %get-tuple-element.16), channel_id=1, source_target_pairs={{4,8},{12,16},{20,24},{8,4},{16,12},{24,20},{5,9},{13,17},{21,25},... | collective-permute-start | bytes 6152 | tf_op jit(solution)/shard_map/ppermute | solution.py:257
  13.9 16.1 %all-to-all-start.1 = ((f32[32,16,128]{2,1,0:T(8,128)}), f32[32,16,128]{2,1,0:T(8,128)S(1)}, u32[]{:S(2)}, u32[]{:S(2)}) async-start(f32[32,16,128]{2,1,0:T(8,128)} %bitcast.3), calls=%async_computation.1 | async-start | bytes 524288 | tf_op jit(solution)/shard_map/all_to_all | solution.py:275
  19.9 7.9 %collective-permute-start.2 = (f32[32,256]{1,0:T(8,128)S(1)}, f32[32,256]{1,0:T(8,128)S(1)}, u32[]{:S(2)}, u32[]{:S(2)}) collective-permute-start(f32[32,256]{1,0:T(8,128)S(1)} %get-tuple-element.17), channel_id=1, source_target_pairs={{4,8},{12,16},{20,24},{8,4},{16,12},{24,20},{5,9},{13,17},{21,25},... | collective-permute-start | bytes 98312 | tf_op jit(solution)/shard_map/ppermute | solution.py:287
  20.6 7.2 %collective-permute-start.3 = (f32[32,256]{1,0:T(8,128)S(1)}, f32[32,256]{1,0:T(8,128)S(1)}, u32[]{:S(2)}, u32[]{:S(2)}) collective-permute-start(f32[32,256]{1,0:T(8,128)S(1)} %get-tuple-element.18), channel_id=1, source_target_pairs={{0,4},{8,12},{16,20},{24,28},{4,0},{12,8},{20,16},{28,24},{1,5},{9... | collective-permute-start | bytes 98312 | tf_op jit(solution)/shard_map/ppermute | solution.py:288
